TPU v7x, 512 devices: a whole 4x8x8 slice. The times are simulated.
512 devices in a mesh: layer: 32 (over z, x), panel: 16 (over y, core).
Axes of the slice: x: 4, y: 8, z: 8, core: 2. Of those that a mesh axis runs over, the one named last changes fastest.
Arguments:
- lower_blocks: bfloat16 [32, 512, 512], P('layer', 'panel'), may hold values from -2 to 0.5
- diag_blocks: bfloat16 [32, 512, 512], P('layer', 'panel'), may hold values from -0.5 to 4, as said below
- upper_blocks: bfloat16 [32, 512, 512], P('layer', 'panel'), may hold values from -2 to 0.5
- right_sides: bfloat16 [32, 512, 128], P('layer', 'panel'), may hold values from -6 to 6
Outputs:
- reduced_diag: bfloat16 [32, 512, 512], P('layer', 'panel')
- reduced_rhs: bfloat16 [32, 512, 128], P('layer', 'panel')
Inputs may be any that keep to these rules, and one draw needn't show every extreme that they name: `diag_blocks`: the diagonal entries of every diagonal block lie between 2 and 4.
All inputs are finite; a program needn't handle non-finite values.
Results may differ from a plain program's by a relative error of at most 0.035.
Values may be sent and summed in bfloat16 or wider, within the bound.
No kernel may reach another device: no remote copies, remote signals or barrier semaphores. Data moves between devices by JAX's collectives and lax.ppermute only.
A program may use at most 64 MiB of HBM per device.

v0:
```python
import jax
import jax.numpy as jnp
from jax import lax
from jax.sharding import Mesh
from jax.sharding import PartitionSpec as P

LEVELS = 3
PANEL = ("panel_0", "panel_1")


def from_everyone(shard, axis):
    size = lax.axis_size(axis)
    return lax.all_to_all(
        jnp.broadcast_to(shard[None], (size, *shard.shape)), axis, 0, 0, tiled=True
    )


def in_order(parts, dim):
    parts = jnp.moveaxis(parts, 0, dim)
    dims = parts.shape
    return parts.reshape(*dims[:dim], dims[dim] * dims[dim + 1], *dims[dim + 2 :])


def gather_axes(shard, axes, dim):
    far, near = axes
    initial = from_everyone(shard, far)
    parts = jnp.swapaxes(from_everyone(initial, near), 0, 1)
    return in_order(parts.reshape(-1, *shard.shape), dim)


def in_one_piece(arrays, axis, dim, along):
    both = jnp.concatenate(arrays, axis=along)
    result, at, gathered = (gather_axes(both, axis, dim), 0, [])
    for a in arrays:
        gathered.append(lax.slice_in_dim(result, at, at + a.shape[along], axis=along))
        at += a.shape[along]
    return tuple(gathered)


def from_behind(shard, axis, by):
    size = lax.axis_size(axis)
    pairs = [(i, i + by) for i in range(size) if 0 <= i + by < size]
    return lax.ppermute(shard, axis, pairs)


def start_inverse(diag_block):
    inverse_diag = 1.0 / jnp.diagonal(diag_block).astype(jnp.float32)
    identity = jnp.eye(diag_block.shape[0], dtype=jnp.float32)
    guess = (
        2.0 * identity * inverse_diag[:, None]
        - inverse_diag[:, None] * diag_block.astype(jnp.float32) * inverse_diag[None, :]
    )
    return guess.astype(jnp.bfloat16)


def eliminate(diag_rows, rhs_rows, terms_left, terms_right, order_size):
    new_lower = (-terms_left[..., :order_size]).astype(jnp.bfloat16)
    new_diag = (
        diag_rows.astype(jnp.float32)
        - terms_left[..., order_size : 2 * order_size]
        - terms_right[..., :order_size]
    ).astype(jnp.bfloat16)
    new_upper = (-terms_right[..., order_size : 2 * order_size]).astype(jnp.bfloat16)
    new_rhs = (
        rhs_rows.astype(jnp.float32)
        - terms_left[..., 2 * order_size :]
        - terms_right[..., 2 * order_size :]
    ).astype(jnp.bfloat16)
    return (new_lower, new_diag, new_upper, new_rhs)


def on_device(lower_blocks, diag_blocks, upper_blocks, right_sides):
    lower_rows = lower_blocks[0]
    diag_rows = diag_blocks[0]
    upper_rows = upper_blocks[0]
    rhs_rows = right_sides[0]
    order_size = lower_rows.shape[1]
    for level_index in range(LEVELS):
        reach = 2**level_index
        full_diag, full_lower, full_upper, full_rhs = in_one_piece(
            (diag_rows, lower_rows, upper_rows, rhs_rows), ("panel_0", "panel_1"), 0, 1
        )
        stacked = jnp.concatenate([full_lower, full_upper, full_rhs], axis=1)
        guess_full = start_inverse(full_diag)
        product = jnp.dot(guess_full, full_diag, preferred_element_type=jnp.float32).astype(
            jnp.bfloat16
        )
        inverse = (
            2.0 * guess_full.astype(jnp.float32)
            - jnp.dot(product, guess_full, preferred_element_type=jnp.float32)
        ).astype(jnp.bfloat16)
        solved = jnp.dot(inverse, stacked, preferred_element_type=jnp.float32).astype(jnp.bfloat16)
        coupling_next = from_behind(lower_rows, "layer", -reach)
        coupling_prev = from_behind(upper_rows, "layer", reach)
        partial_next = jnp.dot(coupling_next, solved, preferred_element_type=jnp.float32)
        partial_prev = jnp.dot(coupling_prev, solved, preferred_element_type=jnp.float32)
        terms_left = from_behind(partial_next.astype(jnp.bfloat16), "layer", reach).astype(
            partial_next.dtype
        )
        terms_right = from_behind(partial_prev.astype(jnp.bfloat16), "layer", -reach).astype(
            partial_prev.dtype
        )
        lower_rows, diag_rows, upper_rows, rhs_rows = eliminate(
            diag_rows, rhs_rows, terms_left, terms_right, order_size
        )
    return (diag_rows[None], rhs_rows[None])


def solution(mesh):
    finer = Mesh(mesh.devices.reshape(mesh.shape["layer"], 8, 2), ("layer", "panel_0", "panel_1"))
    placed = (
        P("layer", PANEL, None),
        P("layer", PANEL, None),
        P("layer", PANEL, None),
        P("layer", PANEL, None),
    )
    return jax.shard_map(
        on_device,
        mesh=finer,
        in_specs=placed,
        out_specs=(P("layer", PANEL, None), P("layer", PANEL, None)),
        check_vma=False,
    )
```

profile of v0, /device:TPU:132, one launch (start us, length us, event | category | flops | bytes accessed | tf_op | source)
XLA Modules:
  0.0 173.1 jit_solution(13344131606839076248)
XLA Ops:
  2.5 7.1 %all-to-all-start = ((bf16[8,32,1664]{2,1,0:T(8,128)(2,1)}), bf16[8,32,1664]{2,1,0:T(8,128)(2,1)S(1)}, u32[]{:S(2)}, u32[]{:S(2)}) async-start(bf16[8,32,1664]{2,1,0:T(8,128)(2,1)} %broadcast_in_dim.24), calls=%async_computation | async-start | bytes 1703936 | tf_op jit(solution)/shard_map/all_to_all | solution.py:13
  9.6 2.4 %collective-permute-start = (bf16[32,512]{1,0:T(8,128)(2,1)S(1)}, bf16[32,512]{1,0:T(8,128)(2,1)S(1)}, u32[]{:S(2)}, u32[]{:S(2)}) collective-permute-start(bf16[32,512]{1,0:T(8,128)(2,1)S(1)} %bitcast.55), channel_id=1, source_target_pairs={{16,0},{32,16},{48,32},{64,48},{80,64},{96,80},{112,96},{128,112},... | collective-permute-start | bytes 98312 | tf_op jit(solution)/shard_map/ppermute | solution.py:43
  12.0 3.4 %collective-permute-start.2 = (bf16[32,512]{1,0:T(8,128)(2,1)S(1)}, bf16[32,512]{1,0:T(8,128)(2,1)S(1)}, u32[]{:S(2)}, u32[]{:S(2)}) collective-permute-start(bf16[32,512]{1,0:T(8,128)(2,1)S(1)} %bitcast.53), channel_id=1, source_target_pairs={{0,16},{16,32},{32,48},{48,64},{64,80},{80,96},{96,112},{112,128},... | collective-permute-start | bytes 98312 | tf_op jit(solution)/shard_map/ppermute | solution.py:43
  15.4 18.6 %all-to-all-done = bf16[8,32,1664]{2,1,0:T(8,128)(2,1)S(1)} async-done(((bf16[8,32,1664]{2,1,0:T(8,128)(2,1)}), bf16[8,32,1664]{2,1,0:T(8,128)(2,1)S(1)}, u32[]{:S(2)}, u32[]{:S(2)}) %all-to-all-start) | async-done | bytes 852000 | tf_op jit(solution)/shard_map/all_to_all | solution.py:13
  34.2 5.1 %all_to_all.30 = bf16[2,8,32,1664]{3,2,1,0:T(8,128)(2,1)S(1)} all-to-all(bf16[2,8,32,1664]{3,2,1,0:T(8,128)(2,1)S(1)} %broadcast_in_dim.25), channel_id=1, replica_groups=mesh['layer'=32,'panel_0'=8,'panel_1'=2] {'panel_1'}, dimensions={0} | all-to-all | bytes 3407872 | tf_op jit(solution)/shard_map/all_to_all | solution.py:13
  39.5 4.8 %gather_fusion = bf16[512]{0:T(512)(128)(2,1)S(1)} fusion(bf16[512,512]{1,0:T(8,128)(2,1)S(1)} %slice.103, s32[512]{0:T(512)S(1)} %bitcast.36), kind=kCustom, calls=%fused_computation | custom fusion | bytes 6144 | tf_op jit(solution)/shard_map/jit(diagonal)/cond/branch_0_fun/gather | solution.py:47
  46.6 2.4 %collective-permute-start.3 = (bf16[32,1152]{1,0:T(8,128)(2,1)S(1)}, bf16[32,1152]{1,0:T(8,128)(2,1)S(1)}, u32[]{:S(2)}, u32[]{:S(2)}) collective-permute-start(bf16[32,1152]{1,0:T(8,128)(2,1)S(1)} %fusion.1), channel_id=1, source_target_pairs={{16,0},{32,16},{48,32},{64,48},{80,64},{96,80},{112,96},{128,112},... | collective-permute-start | bytes 221192 | tf_op jit(solution)/shard_map/ppermute | solution.py:43
  49.4 3.4 %collective-permute-start.1 = (bf16[32,1152]{1,0:T(8,128)(2,1)S(1)}, bf16[32,1152]{1,0:T(8,128)(2,1)S(1)}, u32[]{:S(2)}, u32[]{:S(2)}) collective-permute-start(bf16[32,1152]{1,0:T(8,128)(2,1)S(1)} %fusion), channel_id=1, source_target_pairs={{0,16},{16,32},{32,48},{48,64},{64,80},{80,96},{96,112},{112,128},... | collective-permute-start | bytes 221192 | tf_op jit(solution)/shard_map/ppermute | solution.py:43
  52.9 2.8 %collective-permute-done.1 = bf16[32,1152]{1,0:T(8,128)(2,1)S(1)} collective-permute-done((bf16[32,1152]{1,0:T(8,128)(2,1)S(1)}, bf16[32,1152]{1,0:T(8,128)(2,1)S(1)}, u32[]{:S(2)}, u32[]{:S(2)}) %collective-permute-start.1) | collective-permute-done | bytes 73760 | tf_op jit(solution)/shard_map/ppermute | solution.py:43
  56.7 3.5 %all-to-all-start.2 = ((bf16[8,32,1664]{2,1,0:T(8,128)(2,1)}), bf16[8,32,1664]{2,1,0:T(8,128)(2,1)S(1)}, u32[]{:S(2)}, u32[]{:S(2)}) async-start(bf16[8,32,1664]{2,1,0:T(8,128)(2,1)} %broadcast_in_dim.26), calls=%async_computation.2 | async-start | bytes 1703936 | tf_op jit(solution)/shard_map/all_to_all | solution.py:13
  60.3 5.8 %collective-permute-start.4 = (bf16[32,512]{1,0:T(8,128)(2,1)S(1)}, bf16[32,512]{1,0:T(8,128)(2,1)S(1)}, u32[]{:S(2)}, u32[]{:S(2)}) collective-permute-start(bf16[32,512]{1,0:T(8,128)(2,1)S(1)} %get-tuple-element.6), channel_id=1, source_target_pairs={{32,0},{48,16},{64,32},{80,48},{96,64},{112,80},{128,96},{144,112}... | collective-permute-start | bytes 98312 | tf_op jit(solution)/shard_map/ppermute | solution.py:43
  66.1 3.7 %collective-permute-start.6 = (bf16[32,512]{1,0:T(8,128)(2,1)S(1)}, bf16[32,512]{1,0:T(8,128)(2,1)S(1)}, u32[]{:S(2)}, u32[]{:S(2)}) collective-permute-start(bf16[32,512]{1,0:T(8,128)(2,1)S(1)} %get-tuple-element.7), channel_id=1, source_target_pairs={{0,32},{16,48},{32,64},{48,80},{64,96},{80,112},{96,128},{112,144}... | collective-permute-start | bytes 98312 | tf_op jit(solution)/shard_map/ppermute | solution.py:43
  69.9 14.0 %all-to-all-done.2 = bf16[8,32,1664]{2,1,0:T(8,128)(2,1)S(1)} async-done(((bf16[8,32,1664]{2,1,0:T(8,128)(2,1)}), bf16[8,32,1664]{2,1,0:T(8,128)(2,1)S(1)}, u32[]{:S(2)}, u32[]{:S(2)}) %all-to-all-start.2) | async-done | bytes 852000 | tf_op jit(solution)/shard_map/all_to_all | solution.py:13
  84.0 5.1 %all_to_all.31 = bf16[2,8,32,1664]{3,2,1,0:T(8,128)(2,1)S(1)} all-to-all(bf16[2,8,32,1664]{3,2,1,0:T(8,128)(2,1)S(1)} %broadcast_in_dim.27), channel_id=1, replica_groups=mesh['layer'=32,'panel_0'=8,'panel_1'=2] {'panel_1'}, dimensions={0} | all-to-all | bytes 3407872 | tf_op jit(solution)/shard_map/all_to_all | solution.py:13
  89.3 4.8 %gather_fusion.1 = bf16[512]{0:T(512)(128)(2,1)S(1)} fusion(bf16[512,512]{1,0:T(8,128)(2,1)S(1)} %slice.111, s32[512]{0:T(512)S(1)} %bitcast.37), kind=kCustom, calls=%fused_computation.1 | custom fusion | bytes 6144 | tf_op jit(solution)/shard_map/jit(diagonal)/cond/branch_0_fun/gather | solution.py:47
  98.2 7.6 %collective-permute-start.5 = (bf16[32,1152]{1,0:T(8,128)(2,1)S(1)}, bf16[32,1152]{1,0:T(8,128)(2,1)S(1)}, u32[]{:S(2)}, u32[]{:S(2)}) collective-permute-start(bf16[32,1152]{1,0:T(8,128)(2,1)S(1)} %convolution_convert_fusion.8), channel_id=1, source_target_pairs={{0,32},{16,48},{32,64},{48,80},{64,96},{80,112},{96,128},{112,144}... | collective-permute-start | bytes 221192 | tf_op jit(solution)/shard_map/ppermute | solution.py:43
  108.2 6.7 %collective-permute-done.7 = bf16[32,1152]{1,0:T(8,128)(2,1)S(1)} collective-permute-done((bf16[32,1152]{1,0:T(8,128)(2,1)S(1)}, bf16[32,1152]{1,0:T(8,128)(2,1)S(1)}, u32[]{:S(2)}, u32[]{:S(2)}) %collective-permute-start.7) | collective-permute-done | bytes 73760 | tf_op jit(solution)/shard_map/ppermute | solution.py:43
  115.9 3.5 %all-to-all-start.4 = ((bf16[8,32,1664]{2,1,0:T(8,128)(2,1)}), bf16[8,32,1664]{2,1,0:T(8,128)(2,1)S(1)}, u32[]{:S(2)}, u32[]{:S(2)}) async-start(bf16[8,32,1664]{2,1,0:T(8,128)(2,1)} %broadcast_in_dim.28), calls=%async_computation.4 | async-start | bytes 1703936 | tf_op jit(solution)/shard_map/all_to_all | solution.py:13
  121.4 7.9 %collective-permute-start.10 = (bf16[32,512]{1,0:T(8,128)(2,1)S(1)}, bf16[32,512]{1,0:T(8,128)(2,1)S(1)}, u32[]{:S(2)}, u32[]{:S(2)}) collective-permute-start(bf16[32,512]{1,0:T(8,128)(2,1)S(1)} %get-tuple-element.4), channel_id=1, source_target_pairs={{0,64},{16,80},{32,96},{48,112},{64,128},{80,144},{96,160},{112,17... | collective-permute-start | bytes 98312 | tf_op jit(solution)/shard_map/ppermute | solution.py:43
  129.3 13.7 %all-to-all-done.4 = bf16[8,32,1664]{2,1,0:T(8,128)(2,1)S(1)} async-done(((bf16[8,32,1664]{2,1,0:T(8,128)(2,1)}), bf16[8,32,1664]{2,1,0:T(8,128)(2,1)S(1)}, u32[]{:S(2)}, u32[]{:S(2)}) %all-to-all-start.4) | async-done | bytes 852000 | tf_op jit(solution)/shard_map/all_to_all | solution.py:13
  143.2 5.1 %all_to_all.32 = bf16[2,8,32,1664]{3,2,1,0:T(8,128)(2,1)S(1)} all-to-all(bf16[2,8,32,1664]{3,2,1,0:T(8,128)(2,1)S(1)} %broadcast_in_dim.29), channel_id=1, replica_groups=mesh['layer'=32,'panel_0'=8,'panel_1'=2] {'panel_1'}, dimensions={0} | all-to-all | bytes 3407872 | tf_op jit(solution)/shard_map/all_to_all | solution.py:13
  148.5 4.8 %gather_fusion.2 = bf16[512]{0:T(512)(128)(2,1)S(1)} fusion(bf16[512,512]{1,0:T(8,128)(2,1)S(1)} %slice.119, s32[512]{0:T(512)S(1)} %bitcast.38), kind=kCustom, calls=%fused_computation.2 | custom fusion | bytes 6144 | tf_op jit(solution)/shard_map/jit(diagonal)/cond/branch_0_fun/gather | solution.py:47
  157.4 7.9 %collective-permute-start.9 = (bf16[32,1152]{1,0:T(8,128)(2,1)S(1)}, bf16[32,1152]{1,0:T(8,128)(2,1)S(1)}, u32[]{:S(2)}, u32[]{:S(2)}) collective-permute-start(bf16[32,1152]{1,0:T(8,128)(2,1)S(1)} %convolution_convert_fusion.6), channel_id=1, source_target_pairs={{0,64},{16,80},{32,96},{48,112},{64,128},{80,144},{96,160},{112,17... | collective-permute-start | bytes 221192 | tf_op jit(solution)/shard_map/ppermute | solution.py:43
  167.6 4.3 %collective-permute-done.11 = bf16[32,1152]{1,0:T(8,128)(2,1)S(1)} collective-permute-done((bf16[32,1152]{1,0:T(8,128)(2,1)S(1)}, bf16[32,1152]{1,0:T(8,128)(2,1)S(1)}, u32[]{:S(2)}, u32[]{:S(2)}) %collective-permute-start.11) | collective-permute-done | bytes 73760 | tf_op jit(solution)/shard_map/ppermute | solution.py:43
  (63 shorter events, 23.2 us)
Async XLA Ops:
  0.6 11.4 %copy-start.1 = (bf16[1,32,512]{2,1,0:T(8,128)(2,1)S(1)}, bf16[1,32,512]{2,1,0:T(8,128)(2,1)}, u32[]{:S(2)}) copy-start(bf16[1,32,512]{2,1,0:T(8,128)(2,1)} %param.6) | copy-start | bytes 98308
  0.6 8.9 %copy-start.2 = (bf16[1,32,512]{2,1,0:T(8,128)(2,1)S(1)}, bf16[1,32,512]{2,1,0:T(8,128)(2,1)}, u32[]{:S(2)}) copy-start(bf16[1,32,512]{2,1,0:T(8,128)(2,1)} %param.4) | copy-start | bytes 98308
  2.5 31.6 %all-to-all-start = ((bf16[8,32,1664]{2,1,0:T(8,128)(2,1)}), bf16[8,32,1664]{2,1,0:T(8,128)(2,1)S(1)}, u32[]{:S(2)}, u32[]{:S(2)}) async-start(bf16[8,32,1664]{2,1,0:T(8,128)(2,1)} %broadcast_in_dim.24), calls=%async_computation | async-start | bytes 1703936 | tf_op jit(solution)/shard_map/all_to_all | solution.py:13
  9.6 39.5 %collective-permute-start = (bf16[32,512]{1,0:T(8,128)(2,1)S(1)}, bf16[32,512]{1,0:T(8,128)(2,1)S(1)}, u32[]{:S(2)}, u32[]{:S(2)}) collective-permute-start(bf16[32,512]{1,0:T(8,128)(2,1)S(1)} %bitcast.55), channel_id=1, source_target_pairs={{16,0},{32,16},{48,32},{64,48},{80,64},{96,80},{112,96},{128,112},... | collective-permute-start | bytes 98312 | tf_op jit(solution)/shard_map/ppermute | solution.py:43
  12.0 34.3 %collective-permute-start.2 = (bf16[32,512]{1,0:T(8,128)(2,1)S(1)}, bf16[32,512]{1,0:T(8,128)(2,1)S(1)}, u32[]{:S(2)}, u32[]{:S(2)}) collective-permute-start(bf16[32,512]{1,0:T(8,128)(2,1)S(1)} %bitcast.53), channel_id=1, source_target_pairs={{0,16},{16,32},{32,48},{48,64},{64,80},{80,96},{96,112},{112,128},... | collective-permute-start | bytes 98312 | tf_op jit(solution)/shard_map/ppermute | solution.py:43
  46.3 9.4 %copy-start.3 = (bf16[1,32,128]{2,1,0:T(8,128)(2,1)S(1)}, bf16[1,32,128]{2,1,0:T(8,128)(2,1)}, u32[]{:S(2)}) copy-start(bf16[1,32,128]{2,1,0:T(8,128)(2,1)} %param.7) | copy-start | bytes 24580
  46.3 9.4 %copy-start = (bf16[1,32,512]{2,1,0:T(8,128)(2,1)S(1)}, bf16[1,32,512]{2,1,0:T(8,128)(2,1)}, u32[]{:S(2)}) copy-start(bf16[1,32,512]{2,1,0:T(8,128)(2,1)} %param.5) | copy-start | bytes 98308
  46.6 6.3 %collective-permute-start.3 = (bf16[32,1152]{1,0:T(8,128)(2,1)S(1)}, bf16[32,1152]{1,0:T(8,128)(2,1)S(1)}, u32[]{:S(2)}, u32[]{:S(2)}) collective-permute-start(bf16[32,1152]{1,0:T(8,128)(2,1)S(1)} %fusion.1), channel_id=1, source_target_pairs={{16,0},{32,16},{48,32},{64,48},{80,64},{96,80},{112,96},{128,112},... | collective-permute-start | bytes 221192 | tf_op jit(solution)/shard_map/ppermute | solution.py:43
  49.4 6.2 %collective-permute-start.1 = (bf16[32,1152]{1,0:T(8,128)(2,1)S(1)}, bf16[32,1152]{1,0:T(8,128)(2,1)S(1)}, u32[]{:S(2)}, u32[]{:S(2)}) collective-permute-start(bf16[32,1152]{1,0:T(8,128)(2,1)S(1)} %fusion), channel_id=1, source_target_pairs={{0,16},{16,32},{32,48},{48,64},{64,80},{80,96},{96,112},{112,128},... | collective-permute-start | bytes 221192 | tf_op jit(solution)/shard_map/ppermute | solution.py:43
  56.7 27.2 %all-to-all-start.2 = ((bf16[8,32,1664]{2,1,0:T(8,128)(2,1)}), bf16[8,32,1664]{2,1,0:T(8,128)(2,1)S(1)}, u32[]{:S(2)}, u32[]{:S(2)}) async-start(bf16[8,32,1664]{2,1,0:T(8,128)(2,1)} %broadcast_in_dim.26), calls=%async_computation.2 | async-start | bytes 1703936 | tf_op jit(solution)/shard_map/all_to_all | solution.py:13
  60.3 37.7 %collective-permute-start.4 = (bf16[32,512]{1,0:T(8,128)(2,1)S(1)}, bf16[32,512]{1,0:T(8,128)(2,1)S(1)}, u32[]{:S(2)}, u32[]{:S(2)}) collective-permute-start(bf16[32,512]{1,0:T(8,128)(2,1)S(1)} %get-tuple-element.6), channel_id=1, source_target_pairs={{32,0},{48,16},{64,32},{80,48},{96,64},{112,80},{128,96},{144,112}... | collective-permute-start | bytes 98312 | tf_op jit(solution)/shard_map/ppermute | solution.py:43
  66.1 39.8 %collective-permute-start.6 = (bf16[32,512]{1,0:T(8,128)(2,1)S(1)}, bf16[32,512]{1,0:T(8,128)(2,1)S(1)}, u32[]{:S(2)}, u32[]{:S(2)}) collective-permute-start(bf16[32,512]{1,0:T(8,128)(2,1)S(1)} %get-tuple-element.7), channel_id=1, source_target_pairs={{0,32},{16,48},{32,64},{48,80},{64,96},{80,112},{96,128},{112,144}... | collective-permute-start | bytes 98312 | tf_op jit(solution)/shard_map/ppermute | solution.py:43
  98.2 9.9 %collective-permute-start.5 = (bf16[32,1152]{1,0:T(8,128)(2,1)S(1)}, bf16[32,1152]{1,0:T(8,128)(2,1)S(1)}, u32[]{:S(2)}, u32[]{:S(2)}) collective-permute-start(bf16[32,1152]{1,0:T(8,128)(2,1)S(1)} %convolution_convert_fusion.8), channel_id=1, source_target_pairs={{0,32},{16,48},{32,64},{48,80},{64,96},{80,112},{96,128},{112,144}... | collective-permute-start | bytes 221192 | tf_op jit(solution)/shard_map/ppermute | solution.py:43
  106.2 8.7 %collective-permute-start.7 = (bf16[32,1152]{1,0:T(8,128)(2,1)S(1)}, bf16[32,1152]{1,0:T(8,128)(2,1)S(1)}, u32[]{:S(2)}, u32[]{:S(2)}) collective-permute-start(bf16[32,1152]{1,0:T(8,128)(2,1)S(1)} %convolution_convert_fusion.7), channel_id=1, source_target_pairs={{32,0},{48,16},{64,32},{80,48},{96,64},{112,80},{128,96},{144,112}... | collective-permute-start | bytes 221192 | tf_op jit(solution)/shard_map/ppermute | solution.py:43
  115.9 27.1 %all-to-all-start.4 = ((bf16[8,32,1664]{2,1,0:T(8,128)(2,1)}), bf16[8,32,1664]{2,1,0:T(8,128)(2,1)S(1)}, u32[]{:S(2)}, u32[]{:S(2)}) async-start(bf16[8,32,1664]{2,1,0:T(8,128)(2,1)} %broadcast_in_dim.28), calls=%async_computation.4 | async-start | bytes 1703936 | tf_op jit(solution)/shard_map/all_to_all | solution.py:13
  119.4 37.6 %collective-permute-start.8 = (bf16[32,512]{1,0:T(8,128)(2,1)S(1)}, bf16[32,512]{1,0:T(8,128)(2,1)S(1)}, u32[]{:S(2)}, u32[]{:S(2)}) collective-permute-start(bf16[32,512]{1,0:T(8,128)(2,1)S(1)} %get-tuple-element.3), channel_id=1, source_target_pairs={{64,0},{80,16},{96,32},{112,48},{128,64},{144,80},{160,96},{176,11... | collective-permute-start | bytes 98312 | tf_op jit(solution)/shard_map/ppermute | solution.py:43
  121.4 44.0 %collective-permute-start.10 = (bf16[32,512]{1,0:T(8,128)(2,1)S(1)}, bf16[32,512]{1,0:T(8,128)(2,1)S(1)}, u32[]{:S(2)}, u32[]{:S(2)}) collective-permute-start(bf16[32,512]{1,0:T(8,128)(2,1)S(1)} %get-tuple-element.4), channel_id=1, source_target_pairs={{0,64},{16,80},{32,96},{48,112},{64,128},{80,144},{96,160},{112,17... | collective-permute-start | bytes 98312 | tf_op jit(solution)/shard_map/ppermute | solution.py:43
  157.4 10.2 %collective-permute-start.9 = (bf16[32,1152]{1,0:T(8,128)(2,1)S(1)}, bf16[32,1152]{1,0:T(8,128)(2,1)S(1)}, u32[]{:S(2)}, u32[]{:S(2)}) collective-permute-start(bf16[32,1152]{1,0:T(8,128)(2,1)S(1)} %convolution_convert_fusion.6), channel_id=1, source_target_pairs={{0,64},{16,80},{32,96},{48,112},{64,128},{80,144},{96,160},{112,17... | collective-permute-start | bytes 221192 | tf_op jit(solution)/shard_map/ppermute | solution.py:43
  165.6 6.2 %collective-permute-start.11 = (bf16[32,1152]{1,0:T(8,128)(2,1)S(1)}, bf16[32,1152]{1,0:T(8,128)(2,1)S(1)}, u32[]{:S(2)}, u32[]{:S(2)}) collective-permute-start(bf16[32,1152]{1,0:T(8,128)(2,1)S(1)} %convolution_convert_fusion.5), channel_id=1, source_target_pairs={{64,0},{80,16},{96,32},{112,48},{128,64},{144,80},{160,96},{176,11... | collective-permute-start | bytes 221192 | tf_op jit(solution)/shard_map/ppermute | solution.py:43
where the time goes:
time: 174 us; the launch traced here: 173 us
  starting transfers between devices  64.7 us (37%)
  waiting for transfers between devices  60.2 us (35%)
  local copies, waits for them, and re-layouts  18.5 us (11%)
  blocking collectives  15.3 us (9%)
  matrix products  11.2 us (6%)
  other arithmetic  2.24 us (1%)
    ppermute x12, starting transfers between devices, from_behind(): return lax.ppermute(shard, axis, pairs)  50.5 us
    all_to_all x3, waiting for transfers between devices, from_everyone(): lax.all_to_all(jnp.broadcast_to(shard[None], (size, *shard.shape)), axis,...  46.3 us
    all_to_all x3, blocking collectives, from_everyone(): lax.all_to_all(jnp.broadcast_to(shard[None], (size, *shard.shape)), axis,...  15.3 us
    gather x3, local copies, waits for them, and re-layouts, start_inverse(): inverse_diag = 1.0 / jnp.diagonal(diag_block).astype(jnp.float32)  14.6 us
    all_to_all x3, starting transfers between devices, from_everyone(): lax.all_to_all(jnp.broadcast_to(shard[None], (size, *shard.shape)), axis,...  14.2 us
    ppermute x12, waiting for transfers between devices, from_behind(): return lax.ppermute(shard, axis, pairs)  13.8 us
    dot_general x3, matrix products, on_device(): jnp.dot(inverse, stacked, preferred_element_type=jnp.float32)  6.2 us
  transfers between devices with their start and end apart: 15, of which 7 were waited for; matrix products, arithmetic and copies ran while one was open for 15% of the time, Pallas kernels for 0%

commit v1 on v0

v1 whole, which is shorter than its diff:
```python
import jax
import jax.numpy as jnp
from jax import lax
from jax.experimental import pallas as pl
from jax.experimental.pallas import tpu as pltpu
from jax.sharding import Mesh
from jax.sharding import PartitionSpec as P

LAYERS = 32
AXES = ("layer", "chip", "c")


def send(block, by):
    pairs = [(i, i + by) for i in range(LAYERS) if 0 <= i + by < LAYERS]
    return lax.ppermute(block, "layer", pairs)


def swap(block):
    return lax.ppermute(block, "c", [(0, 1), (1, 0)])


def dot(a, b):
    return jnp.dot(a, b, preferred_element_type=jnp.float32)


def dot_across(a, b):
    return lax.dot_general(a, b, (((1,), (1,)), ((), ())), preferred_element_type=jnp.float32)


def half_of(block, core):
    h = block.shape[1] // 2
    return jnp.where(core == 0, block[:, :h], block[:, h:])


def inverse(diag):
    order = diag.shape[0]
    eye = jnp.eye(order, dtype=jnp.bool_)
    wide = diag.astype(jnp.float32)
    picked = jnp.where(eye, wide, 0.0)
    across = 1.0 / jnp.sum(picked, axis=0, keepdims=True)
    down = 1.0 / jnp.sum(picked, axis=1, keepdims=True)
    guess = jnp.where(eye, 2.0 * down, 0.0) - down * wide * across
    guess = guess.astype(jnp.bfloat16)
    product = dot(guess, diag).astype(jnp.bfloat16)
    return (2.0 * guess.astype(jnp.float32) - dot(product, guess)).astype(jnp.bfloat16)


def after(diag, rhs, left, right):
    h, f = diag.shape[1], rhs.shape[1]
    new_diag = diag.astype(jnp.float32) - left[:, h + f :] - right[:, :h]
    new_rhs = rhs.astype(jnp.float32) - left[:, h : h + f] - right[:, h : h + f]
    mine = jnp.concatenate([new_diag, -left[:, :h], -right[:, h + f :]], axis=1)
    return mine.astype(jnp.bfloat16), new_rhs.astype(jnp.bfloat16)


def solve_kernel(core_ref, mine_ref, other_ref, rhs_ref, solved_ref, lower_ref, upper_ref, diag_ref):
    h = diag_ref.shape[1] // 2
    f = rhs_ref.shape[1]
    for own in range(2):

        @pl.when(core_ref[0] == own)
        def _(own=own):
            low, high = (mine_ref, other_ref) if own == 0 else (other_ref, mine_ref)
            for k, whole in enumerate((diag_ref, lower_ref, upper_ref)):
                whole[:, :h] = low[:, k * h : (k + 1) * h]
                whole[:, h:] = high[:, k * h : (k + 1) * h]

    found = inverse(diag_ref[...])

    def solved(right):
        return dot(found, right).T.astype(jnp.bfloat16)

    solved_ref[:h] = solved(mine_ref[:, h : 2 * h])
    solved_ref[h : h + f] = solved(rhs_ref[...])
    solved_ref[h + f :] = solved(mine_ref[:, 2 * h :])


def solve(mine, rhs, core):
    m, f = rhs.shape
    h = m // 2
    square = jax.ShapeDtypeStruct((m, m), jnp.bfloat16)
    whole = pl.BlockSpec(memory_space=pltpu.VMEM)
    return pl.pallas_call(
        solve_kernel,
        out_shape=(jax.ShapeDtypeStruct((m + f, m), jnp.bfloat16), square, square),
        in_specs=[pl.BlockSpec(memory_space=pltpu.SMEM), whole, whole, whole],
        out_specs=(whole, whole, whole),
        scratch_shapes=[pltpu.VMEM((m, m), jnp.bfloat16)],
        compiler_params=pltpu.CompilerParams(vmem_limit_bytes=24 * 2**20),
        cost_estimate=pl.CostEstimate(flops=2 * m * m * (3 * m + f), bytes_accessed=12 * m * m, transcendentals=0),
    )(core.reshape(1).astype(jnp.int32), mine, swap(mine), rhs)


def whole_layer(rows, core):
    copies = jnp.broadcast_to(rows[None], (8, *rows.shape))
    mine = lax.all_to_all(copies, "chip", 0, 0, tiled=True)
    other = swap(mine)
    both = jnp.stack([jnp.where(core == 0, mine, other), jnp.where(core == 0, other, mine)], axis=1)
    return both.reshape(-1, rows.shape[1])


def on_device(lower_blocks, diag_blocks, upper_blocks, right_sides):
    core = lax.axis_index("c")
    m, r = lower_blocks.shape[2], right_sides.shape[2]
    h, f = m // 2, r // 2
    own = (diag_blocks[0], lower_blocks[0], upper_blocks[0], right_sides[0])
    full = whole_layer(jnp.concatenate(own, axis=1), core)
    diag, lower, upper, rhs = full[:, :m], full[:, m : 2 * m], full[:, 2 * m : 3 * m], full[:, 3 * m :]
    wide = jnp.concatenate([half_of(lower, core), half_of(rhs, core), half_of(upper, core)], axis=1)
    solved = dot(inverse(diag), wide).astype(jnp.bfloat16)
    left = dot(lower, send(solved, 1))
    right = dot(upper, send(solved, -1))
    mine, rhs = after(half_of(diag, core), half_of(rhs, core), left, right)
    solved, lower, upper = solve(mine, rhs, core)
    left = dot_across(lower, send(solved, 2))
    right = dot_across(upper, send(solved, -2))
    mine, rhs = after(mine[:, :h], rhs, left, right)
    solved, lower, upper = solve(mine, rhs, core)
    forward = send(solved[h:], 4)
    back = send(solved[: h + f], -4)
    n = 2 * own[0].shape[0]
    at = lax.axis_index("chip") * n

    def rows_of(block):
        return lax.dynamic_slice_in_dim(block, at, n, axis=0)

    left = dot_across(rows_of(lower), forward)
    right = dot_across(rows_of(upper), back)
    new_diag = rows_of(mine[:, :h]).astype(jnp.float32) - left[:, f:] - right[:, :h]
    new_rhs = rows_of(rhs).astype(jnp.float32) - left[:, :f] - right[:, h:]
    done = jnp.concatenate([new_diag, new_rhs], axis=1).astype(jnp.bfloat16)
    done = lax.all_gather(done, "c", axis=0)
    mine = jnp.where(core == 0, done[:, : n // 2], done[:, n // 2 :])
    out_diag = jnp.concatenate([mine[0, :, :h], mine[1, :, :h]], axis=1)
    out_rhs = jnp.concatenate([mine[0, :, h:], mine[1, :, h:]], axis=1)
    return out_diag[None], out_rhs[None]


def solution(mesh):
    finer = Mesh(mesh.devices.reshape(LAYERS, 8, 2), AXES)
    placed = P("layer", ("chip", "c"), None)
    return jax.shard_map(
        on_device,
        mesh=finer,
        in_specs=(placed,) * 4,
        out_specs=(placed,) * 2,
        check_vma=False,
    )
```

time: 174 us -> 133 us (0.76)
  the two profiles are of different devices: /device:TPU:132 before, /device:TPU:71 now
where the time goes in v1:
time: 133 us; the launch traced here: 132 us
  waiting for transfers between devices  57.9 us (44%)
  blocking collectives  32.4 us (24%)
  starting transfers between devices  29.6 us (22%)
  matrix products  4.56 us (3%)
  other arithmetic  3.94 us (3%)
  Pallas kernels  3.07 us (2%)
    ppermute x6, waiting for transfers between devices, send(): return lax.ppermute(block, 'layer', pairs)  52.3 us
    all_to_all x1, blocking collectives, whole_layer(): mine = lax.all_to_all(copies, 'chip', 0, 0, tiled=True)  29.7 us
    ppermute x6, starting transfers between devices, send(): return lax.ppermute(block, 'layer', pairs)  19.4 us
    ppermute x3, starting transfers between devices, swap(): return lax.ppermute(block, 'c', [(0, 1), (1, 0)])  10.1 us
    ppermute x3, waiting for transfers between devices, swap(): return lax.ppermute(block, 'c', [(0, 1), (1, 0)])  5.57 us
    pallas_call x2, Pallas kernels, solve(): pl.pallas_call(solve_kernel, out_shape=(jax.ShapeDtypeStruct((m + f, m),...  3.07 us
    dot_general x4, matrix products, dot(): return jnp.dot(a, b, preferred_element_type=jnp.float32)  2.92 us
    all_gather x1, blocking collectives, on_device(): done = lax.all_gather(done, 'c', axis=0)  2.73 us
  transfers between devices with their start and end apart: 9, of which 9 were waited for; matrix products, arithmetic and copies ran while one was open for 1% of the time, Pallas kernels for 0%

profile of v1, /device:TPU:71, one launch (start us, length us, event | category | flops | bytes accessed | tf_op | source)
XLA Modules:
  0.0 132.5 jit_solution(7097173946771380978)
XLA Ops:
  0.6 0.8 pad_maximum_fusion.3
  1.5 29.7 %all_to_all.5 = bf16[8,32,1664]{2,1,0:T(8,128)(2,1)S(1)} all-to-all(bf16[8,32,1664]{2,1,0:T(8,128)(2,1)S(1)} %broadcast_in_dim.28), channel_id=1, replica_groups=mesh['layer'=32,'chip'=8,'c'=2] {'chip'}, dimensions={0} | all-to-all | bytes 1703936 | tf_op jit(solution)/shard_map/all_to_all | solution.py:96
  31.2 4.3 %collective-permute-start = (bf16[8,32,1664]{2,1,0:T(8,128)(2,1)S(1)}, bf16[8,32,1664]{2,1,0:T(8,128)(2,1)S(1)}, u32[]{:S(2)}, u32[]{:S(2)}) collective-permute-start(bf16[8,32,1664]{2,1,0:T(8,128)(2,1)S(1)} %all_to_all.5), channel_id=1, source_target_pairs={{0,1},{1,0},{2,3},{3,2},{4,5},{5,4},{6,7},{7,6},{8,9},{9,8},{10,11... | collective-permute-start | bytes 2555912 | tf_op jit(solution)/shard_map/ppermute | solution.py:19
  35.5 2.0 %collective-permute-done = bf16[8,32,1664]{2,1,0:T(8,128)(2,1)S(1)} collective-permute-done((bf16[8,32,1664]{2,1,0:T(8,128)(2,1)S(1)}, bf16[8,32,1664]{2,1,0:T(8,128)(2,1)S(1)}, u32[]{:S(2)}, u32[]{:S(2)}) %collective-permute-start) | collective-permute-done | bytes 852000 | tf_op jit(solution)/shard_map/ppermute | solution.py:19
  38.7 1.2 convolution_convert_fusion
  39.9 3.9 %collective-permute-start.1 = (bf16[512,576]{0,1:T(8,128)(2,1)S(1)}, bf16[512,576]{0,1:T(8,128)(2,1)S(1)}, u32[]{:S(2)}, u32[]{:S(2)}) collective-permute-start(bf16[512,576]{0,1:T(8,128)(2,1)S(1)} %convolution_convert_fusion), channel_id=1, source_target_pairs={{0,16},{16,32},{32,48},{48,64},{64,80},{80,96},{96,112},{112,128},... | collective-permute-start | bytes 1769480 | tf_op jit(solution)/shard_map/ppermute | solution.py:15
  43.8 1.9 %collective-permute-start.2 = (bf16[512,576]{0,1:T(8,128)(2,1)S(1)}, bf16[512,576]{0,1:T(8,128)(2,1)S(1)}, u32[]{:S(2)}, u32[]{:S(2)}) collective-permute-start(bf16[512,576]{0,1:T(8,128)(2,1)S(1)} %convolution_convert_fusion), channel_id=1, source_target_pairs={{16,0},{32,16},{48,32},{64,48},{80,64},{96,80},{112,96},{128,112},... | collective-permute-start | bytes 1769480 | tf_op jit(solution)/shard_map/ppermute | solution.py:15
  45.7 10.6 %collective-permute-done.1 = bf16[512,576]{0,1:T(8,128)(2,1)S(1)} collective-permute-done((bf16[512,576]{0,1:T(8,128)(2,1)S(1)}, bf16[512,576]{0,1:T(8,128)(2,1)S(1)}, u32[]{:S(2)}, u32[]{:S(2)}) %collective-permute-start.1) | collective-permute-done | bytes 589856 | tf_op jit(solution)/shard_map/ppermute | solution.py:15
  56.9 5.1 %collective-permute-done.2 = bf16[512,576]{0,1:T(8,128)(2,1)S(1)} collective-permute-done((bf16[512,576]{0,1:T(8,128)(2,1)S(1)}, bf16[512,576]{0,1:T(8,128)(2,1)S(1)}, u32[]{:S(2)}, u32[]{:S(2)}) %collective-permute-start.2) | collective-permute-done | bytes 589856 | tf_op jit(solution)/shard_map/ppermute | solution.py:15
  63.1 3.4 %collective-permute-start.3 = (bf16[512,768]{1,0:T(8,128)(2,1)S(1)}, bf16[512,768]{1,0:T(8,128)(2,1)S(1)}, u32[]{:S(2)}, u32[]{:S(2)}) collective-permute-start(bf16[512,768]{1,0:T(8,128)(2,1)S(1)} %pad_maximum_fusion.1.mine_ref), channel_id=1, source_target_pairs={{0,1},{1,0},{2,3},{3,2},{4,5},{5,4},{6,7},{7,6},{8,9},{9,8},{10,11... | collective-permute-start | bytes 2359304 | tf_op jit(solution)/shard_map/ppermute | solution.py:19
  66.7 1.8 %collective-permute-done.3.other_ref = bf16[512,768]{1,0:T(8,128)(2,1)S(1)} collective-permute-done((bf16[512,768]{1,0:T(8,128)(2,1)S(1)}, bf16[512,768]{1,0:T(8,128)(2,1)S(1)}, u32[]{:S(2)}, u32[]{:S(2)}) %collective-permute-start.3) | collective-permute-done | bytes 786464 | tf_op jit(solution)/shard_map/ppermute | solution.py:19
  68.4 1.5 %shard_map.59 = (bf16[576,512]{1,0:T(8,128)(2,1)S(1)}, bf16[512,512]{1,0:T(8,128)(2,1)S(1)}, bf16[512,512]{1,0:T(8,128)(2,1)S(1)}) custom-call(s32[1]{0:T(128)} %bitcast.8.core_ref, bf16[512,768]{1,0:T(8,128)(2,1)S(1)} %pad_maximum_fusion.1.mine_ref, bf16[512,768]{1,0:T(8,128)(2,1)S(1)} %collective-permute-done.3.other_ref, bf16[512,64]{1,0:T(8,128)(2,1)S(1)} %fusion.26.rhs_ref), custom_call_target="tpu_custom_call" | custom-call | flops 838860800 | bytes 3145728 | tf_op jit(solution)/shard_map/pallas_call | solution.py:83
  70.0 1.9 %collective-permute-start.5 = (bf16[576,512]{1,0:T(8,128)(2,1)S(1)}, bf16[576,512]{1,0:T(8,128)(2,1)S(1)}, u32[]{:S(2)}, u32[]{:S(2)}) collective-permute-start(bf16[576,512]{1,0:T(8,128)(2,1)S(1)} %get-tuple-element.9), channel_id=1, source_target_pairs={{32,0},{48,16},{64,32},{80,48},{96,64},{112,80},{128,96},{144,112}... | collective-permute-start | bytes 1769480 | tf_op jit(solution)/shard_map/ppermute | solution.py:15
  71.9 5.8 %collective-permute-start.4 = (bf16[576,512]{1,0:T(8,128)(2,1)S(1)}, bf16[576,512]{1,0:T(8,128)(2,1)S(1)}, u32[]{:S(2)}, u32[]{:S(2)}) collective-permute-start(bf16[576,512]{1,0:T(8,128)(2,1)S(1)} %get-tuple-element.9), channel_id=1, source_target_pairs={{0,32},{16,48},{32,64},{48,80},{64,96},{80,112},{96,128},{112,144}... | collective-permute-start | bytes 1769480 | tf_op jit(solution)/shard_map/ppermute | solution.py:15
  77.7 19.5 %collective-permute-done.5 = bf16[576,512]{1,0:T(8,128)(2,1)S(1)} collective-permute-done((bf16[576,512]{1,0:T(8,128)(2,1)S(1)}, bf16[576,512]{1,0:T(8,128)(2,1)S(1)}, u32[]{:S(2)}, u32[]{:S(2)}) %collective-permute-start.5) | collective-permute-done | bytes 589856 | tf_op jit(solution)/shard_map/ppermute | solution.py:15
  97.8 4.4 %collective-permute-done.4 = bf16[576,512]{1,0:T(8,128)(2,1)S(1)} collective-permute-done((bf16[576,512]{1,0:T(8,128)(2,1)S(1)}, bf16[576,512]{1,0:T(8,128)(2,1)S(1)}, u32[]{:S(2)}, u32[]{:S(2)}) %collective-permute-start.4) | collective-permute-done | bytes 589856 | tf_op jit(solution)/shard_map/ppermute | solution.py:15
  103.2 2.4 %collective-permute-start.6 = (bf16[512,768]{1,0:T(8,128)(2,1)S(1)}, bf16[512,768]{1,0:T(8,128)(2,1)S(1)}, u32[]{:S(2)}, u32[]{:S(2)}) collective-permute-start(bf16[512,768]{1,0:T(8,128)(2,1)S(1)} %pad_maximum_fusion.2.mine_ref), channel_id=1, source_target_pairs={{0,1},{1,0},{2,3},{3,2},{4,5},{5,4},{6,7},{7,6},{8,9},{9,8},{10,11... | collective-permute-start | bytes 2359304 | tf_op jit(solution)/shard_map/ppermute | solution.py:19
  105.7 1.8 %collective-permute-done.6.other_ref = bf16[512,768]{1,0:T(8,128)(2,1)S(1)} collective-permute-done((bf16[512,768]{1,0:T(8,128)(2,1)S(1)}, bf16[512,768]{1,0:T(8,128)(2,1)S(1)}, u32[]{:S(2)}, u32[]{:S(2)}) %collective-permute-start.6) | collective-permute-done | bytes 786464 | tf_op jit(solution)/shard_map/ppermute | solution.py:19
  107.5 1.5 %shard_map.60 = (bf16[576,512]{1,0:T(8,128)(2,1)S(1)}, bf16[512,512]{1,0:T(8,128)(2,1)S(1)}, bf16[512,512]{1,0:T(8,128)(2,1)S(1)}) custom-call(s32[1]{0:T(128)} %bitcast.8.core_ref, bf16[512,768]{1,0:T(8,128)(2,1)S(1)} %pad_maximum_fusion.2.mine_ref, bf16[512,768]{1,0:T(8,128)(2,1)S(1)} %collective-permute-done.6.other_ref, bf16[512,64]{1,0:T(8,128)(2,1)S(1)} %fusion.25.rhs_ref), custom_call_target="tpu_custom_call" | custom-call | flops 838860800 | bytes 3145728 | tf_op jit(solution)/shard_map/pallas_call | solution.py:83
  109.1 4.0 %collective-permute-start.7 = (bf16[320,512]{1,0:T(8,128)(2,1)S(1)}, bf16[320,512]{1,0:T(8,128)(2,1)S(1)}, u32[]{:S(2)}, u32[]{:S(2)}) collective-permute-start(bf16[320,512]{1,0:T(8,128)(2,1)S(1)} %get-tuple-element.28), channel_id=1, source_target_pairs={{0,64},{16,80},{32,96},{48,112},{64,128},{80,144},{96,160},{112,17... | collective-permute-start | bytes 983048 | tf_op jit(solution)/shard_map/ppermute | solution.py:15
  113.1 1.9 %collective-permute-start.8 = (bf16[320,512]{1,0:T(8,128)(2,1)S(1)}, bf16[320,512]{1,0:T(8,128)(2,1)S(1)}, u32[]{:S(2)}, u32[]{:S(2)}) collective-permute-start(bf16[320,512]{1,0:T(8,128)(2,1)S(1)} %get-tuple-element.29), channel_id=1, source_target_pairs={{64,0},{80,16},{96,32},{112,48},{128,64},{144,80},{160,96},{176,11... | collective-permute-start | bytes 983048 | tf_op jit(solution)/shard_map/ppermute | solution.py:15
  115.1 4.9 %collective-permute-done.7 = bf16[320,512]{1,0:T(8,128)(2,1)S(1)} collective-permute-done((bf16[320,512]{1,0:T(8,128)(2,1)S(1)}, bf16[320,512]{1,0:T(8,128)(2,1)S(1)}, u32[]{:S(2)}, u32[]{:S(2)}) %collective-permute-start.7) | collective-permute-done | bytes 327712 | tf_op jit(solution)/shard_map/ppermute | solution.py:15
  120.2 7.9 %collective-permute-done.8 = bf16[320,512]{1,0:T(8,128)(2,1)S(1)} collective-permute-done((bf16[320,512]{1,0:T(8,128)(2,1)S(1)}, bf16[320,512]{1,0:T(8,128)(2,1)S(1)}, u32[]{:S(2)}, u32[]{:S(2)}) %collective-permute-start.8) | collective-permute-done | bytes 327712 | tf_op jit(solution)/shard_map/ppermute | solution.py:15
  128.4 2.7 %all_gather.4 = bf16[2,64,320]{2,1,0:T(8,128)(2,1)S(1)} all-gather(bf16[1,64,320]{2,1,0:T(8,128)(2,1)S(1)} %pad_maximum_fusion.4), channel_id=1, replica_groups=mesh['layer'=32,'chip'=8,'c'=2] {'c'}, dimensions={0}, use_global_device_ids=true | all-gather | bytes 122880 | tf_op jit(solution)/shard_map/all_gather | solution.py:132
  (29 shorter events, 6.6 us)
Async XLA Ops:
  31.2 6.3 %collective-permute-start = (bf16[8,32,1664]{2,1,0:T(8,128)(2,1)S(1)}, bf16[8,32,1664]{2,1,0:T(8,128)(2,1)S(1)}, u32[]{:S(2)}, u32[]{:S(2)}) collective-permute-start(bf16[8,32,1664]{2,1,0:T(8,128)(2,1)S(1)} %all_to_all.5), channel_id=1, source_target_pairs={{0,1},{1,0},{2,3},{3,2},{4,5},{5,4},{6,7},{7,6},{8,9},{9,8},{10,11... | collective-permute-start | bytes 2555912 | tf_op jit(solution)/shard_map/ppermute | solution.py:19
  39.9 16.4 %collective-permute-start.1 = (bf16[512,576]{0,1:T(8,128)(2,1)S(1)}, bf16[512,576]{0,1:T(8,128)(2,1)S(1)}, u32[]{:S(2)}, u32[]{:S(2)}) collective-permute-start(bf16[512,576]{0,1:T(8,128)(2,1)S(1)} %convolution_convert_fusion), channel_id=1, source_target_pairs={{0,16},{16,32},{32,48},{48,64},{64,80},{80,96},{96,112},{112,128},... | collective-permute-start | bytes 1769480 | tf_op jit(solution)/shard_map/ppermute | solution.py:15
  43.8 18.2 %collective-permute-start.2 = (bf16[512,576]{0,1:T(8,128)(2,1)S(1)}, bf16[512,576]{0,1:T(8,128)(2,1)S(1)}, u32[]{:S(2)}, u32[]{:S(2)}) collective-permute-start(bf16[512,576]{0,1:T(8,128)(2,1)S(1)} %convolution_convert_fusion), channel_id=1, source_target_pairs={{16,0},{32,16},{48,32},{64,48},{80,64},{96,80},{112,96},{128,112},... | collective-permute-start | bytes 1769480 | tf_op jit(solution)/shard_map/ppermute | solution.py:15
  63.1 5.3 %collective-permute-start.3 = (bf16[512,768]{1,0:T(8,128)(2,1)S(1)}, bf16[512,768]{1,0:T(8,128)(2,1)S(1)}, u32[]{:S(2)}, u32[]{:S(2)}) collective-permute-start(bf16[512,768]{1,0:T(8,128)(2,1)S(1)} %pad_maximum_fusion.1.mine_ref), channel_id=1, source_target_pairs={{0,1},{1,0},{2,3},{3,2},{4,5},{5,4},{6,7},{7,6},{8,9},{9,8},{10,11... | collective-permute-start | bytes 2359304 | tf_op jit(solution)/shard_map/ppermute | solution.py:19
  70.0 27.2 %collective-permute-start.5 = (bf16[576,512]{1,0:T(8,128)(2,1)S(1)}, bf16[576,512]{1,0:T(8,128)(2,1)S(1)}, u32[]{:S(2)}, u32[]{:S(2)}) collective-permute-start(bf16[576,512]{1,0:T(8,128)(2,1)S(1)} %get-tuple-element.9), channel_id=1, source_target_pairs={{32,0},{48,16},{64,32},{80,48},{96,64},{112,80},{128,96},{144,112}... | collective-permute-start | bytes 1769480 | tf_op jit(solution)/shard_map/ppermute | solution.py:15
  71.9 30.3 %collective-permute-start.4 = (bf16[576,512]{1,0:T(8,128)(2,1)S(1)}, bf16[576,512]{1,0:T(8,128)(2,1)S(1)}, u32[]{:S(2)}, u32[]{:S(2)}) collective-permute-start(bf16[576,512]{1,0:T(8,128)(2,1)S(1)} %get-tuple-element.9), channel_id=1, source_target_pairs={{0,32},{16,48},{32,64},{48,80},{64,96},{80,112},{96,128},{112,144}... | collective-permute-start | bytes 1769480 | tf_op jit(solution)/shard_map/ppermute | solution.py:15
  103.2 4.3 %collective-permute-start.6 = (bf16[512,768]{1,0:T(8,128)(2,1)S(1)}, bf16[512,768]{1,0:T(8,128)(2,1)S(1)}, u32[]{:S(2)}, u32[]{:S(2)}) collective-permute-start(bf16[512,768]{1,0:T(8,128)(2,1)S(1)} %pad_maximum_fusion.2.mine_ref), channel_id=1, source_target_pairs={{0,1},{1,0},{2,3},{3,2},{4,5},{5,4},{6,7},{7,6},{8,9},{9,8},{10,11... | collective-permute-start | bytes 2359304 | tf_op jit(solution)/shard_map/ppermute | solution.py:19
  109.1 10.8 %collective-permute-start.7 = (bf16[320,512]{1,0:T(8,128)(2,1)S(1)}, bf16[320,512]{1,0:T(8,128)(2,1)S(1)}, u32[]{:S(2)}, u32[]{:S(2)}) collective-permute-start(bf16[320,512]{1,0:T(8,128)(2,1)S(1)} %get-tuple-element.28), channel_id=1, source_target_pairs={{0,64},{16,80},{32,96},{48,112},{64,128},{80,144},{96,160},{112,17... | collective-permute-start | bytes 983048 | tf_op jit(solution)/shard_map/ppermute | solution.py:15
  113.1 14.9 %collective-permute-start.8 = (bf16[320,512]{1,0:T(8,128)(2,1)S(1)}, bf16[320,512]{1,0:T(8,128)(2,1)S(1)}, u32[]{:S(2)}, u32[]{:S(2)}) collective-permute-start(bf16[320,512]{1,0:T(8,128)(2,1)S(1)} %get-tuple-element.29), channel_id=1, source_target_pairs={{64,0},{80,16},{96,32},{112,48},{128,64},{144,80},{160,96},{176,11... | collective-permute-start | bytes 983048 | tf_op jit(solution)/shard_map/ppermute | solution.py:15

commit v2 on v1

v2 whole, which is shorter than its diff:
```python
import jax
import jax.numpy as jnp
from jax import lax
from jax.experimental import pallas as pl
from jax.experimental.pallas import tpu as pltpu
from jax.sharding import Mesh
from jax.sharding import PartitionSpec as P

LAYERS = 32
AXES = ("layer", "far", "near", "c")


def send(block, by):
    pairs = [(i, i + by) for i in range(LAYERS) if 0 <= i + by < LAYERS]
    return lax.ppermute(block, "layer", pairs)


def swap(block):
    return lax.ppermute(block, "c", [(0, 1), (1, 0)])


def of_cores(rows):
    return lax.all_gather(rows, "c", axis=0, tiled=True)


def of_pair(rows):
    return lax.all_gather(rows, "near", axis=0, tiled=True)


def dot(a, b):
    return jnp.dot(a, b, preferred_element_type=jnp.float32)


def dot_across(a, b):
    return lax.dot_general(a, b, (((1,), (1,)), ((), ())), preferred_element_type=jnp.float32)


def inverse(diag):
    order = diag.shape[0]
    eye = jnp.eye(order, dtype=jnp.bool_)
    wide = diag.astype(jnp.float32)
    picked = jnp.where(eye, wide, 0.0)
    across = 1.0 / jnp.sum(picked, axis=0, keepdims=True)
    down = 1.0 / jnp.sum(picked, axis=1, keepdims=True)
    guess = jnp.where(eye, 2.0 * down, 0.0) - down * wide * across
    guess = guess.astype(jnp.bfloat16)
    product = dot(guess, diag).astype(jnp.bfloat16)
    return (2.0 * guess.astype(jnp.float32) - dot(product, guess)).astype(jnp.bfloat16)


def solve_kernel(diag_ref, *refs):
    solved_ref = refs[-1]
    found = inverse(diag_ref[...])
    at = 0
    for ref in refs[:-1]:
        rows = ref.shape[0]
        solved_ref[at : at + rows] = dot(ref[...], found).astype(jnp.bfloat16)
        at += rows


def solve(diag, parts):
    m = diag.shape[0]
    rows = sum(p.shape[0] for p in parts)
    whole = pl.BlockSpec(memory_space=pltpu.VMEM)
    return pl.pallas_call(
        solve_kernel,
        out_shape=jax.ShapeDtypeStruct((rows, m), jnp.bfloat16),
        in_specs=[whole] * (1 + len(parts)),
        out_specs=whole,
        compiler_params=pltpu.CompilerParams(vmem_limit_bytes=24 * 2**20),
        cost_estimate=pl.CostEstimate(flops=2 * m * m * (2 * m + rows), bytes_accessed=4 * m * (m + rows), transcendentals=0),
    )(diag, *parts)


def after(diag, rhs, left, right):
    h, f = diag.shape[0], rhs.shape[0]
    new_diag = diag.astype(jnp.float32) - left[h + f :] - right[:h]
    new_rhs = rhs.astype(jnp.float32) - left[h : h + f] - right[h : h + f]
    new = (new_diag, -left[:h], -right[h + f :], new_rhs)
    return tuple(a.astype(jnp.bfloat16) for a in new)


def first_kernel(core_ref, mine_ref, other_ref, solved_ref, lower_ref, upper_ref, diag_out, rhs_out, diag_ref, rhs_ref):
    m = diag_ref.shape[0]
    n = mine_ref.shape[1]
    wholes = ((diag_ref, 0, m), (lower_ref, m, m), (upper_ref, 2 * m, m), (rhs_ref, 3 * m, rhs_ref.shape[1]))
    for own in range(2):

        @pl.when(core_ref[0] == own)
        def _(own=own):
            for k in range(mine_ref.shape[0]):
                for ref, c in ((mine_ref, own), (other_ref, 1 - own)):
                    at = (2 * k + c) * n
                    for whole, left, width in wholes:
                        whole[at : at + n] = ref[k, :, left : left + width]

    found = inverse(diag_ref[...])
    q, g = solved_ref.shape[1] // 4, rhs_out.shape[0]
    for k in range(4):

        @pl.when(core_ref[1] == k)
        def _(k=k):
            side = slice(k * q, k * q + q)
            small = slice(k * g, k * g + g)

            def solved(right):
                return dot(found, right).T.astype(jnp.bfloat16)

            solved_ref[:q] = solved(lower_ref[:, side])
            solved_ref[q + g :] = solved(upper_ref[:, side])
            solved_ref[q : q + g] = solved(rhs_ref[:, small])
            diag_out[...] = diag_ref[:, side].T
            rhs_out[...] = rhs_ref[:, small].T


def first_solve(rows, core, quarter, m):
    copies = jnp.broadcast_to(rows[None], (8, *rows.shape))
    mine = lax.all_to_all(copies, ("far", "near"), 0, 0, tiled=True)
    r = rows.shape[1] - 3 * m
    whole = pl.BlockSpec(memory_space=pltpu.VMEM)
    shapes = (((2 * m + r) // 4, m), (m, m), (m, m), (m // 4, m), (r // 4, m))
    return pl.pallas_call(
        first_kernel,
        out_shape=tuple(jax.ShapeDtypeStruct(s, jnp.bfloat16) for s in shapes),
        in_specs=[pl.BlockSpec(memory_space=pltpu.SMEM), whole, whole],
        out_specs=(whole,) * 5,
        scratch_shapes=[pltpu.VMEM((m, m), jnp.bfloat16), pltpu.VMEM((m, r), jnp.bfloat16)],
        compiler_params=pltpu.CompilerParams(vmem_limit_bytes=24 * 2**20),
        cost_estimate=pl.CostEstimate(flops=7 * m * m * m, bytes_accessed=16 * m * m, transcendentals=0),
    )(jnp.stack([core, quarter]).astype(jnp.int32), mine, swap(mine))


def on_device(lower_blocks, diag_blocks, upper_blocks, right_sides):
    core, near = lax.axis_index("c"), lax.axis_index("near")
    m, r = lower_blocks.shape[2], right_sides.shape[2]
    q, g = m // 4, r // 4
    own = (diag_blocks[0], lower_blocks[0], upper_blocks[0], right_sides[0])
    rows = jnp.concatenate(own, axis=1)
    solved, lower, upper, diag, rhs = first_solve(rows, core, core * 2 + near, m)
    left, right = dot_across(send(solved, 1), lower), dot_across(send(solved, -1), upper)
    diag, lower, upper, rhs = after(diag, rhs, left, right)

    solved = solve(of_cores(of_pair(diag)), (lower, rhs, upper))
    solved, lower, upper = lax.optimization_barrier((solved, lower, upper))
    ahead, behind = send(solved, 2), send(solved, -2)
    both = lax.all_gather(jnp.concatenate([lower, upper], axis=0), "near", axis=0)
    lower = of_cores(jnp.concatenate([both[0, :q], both[1, :q]], axis=0))
    upper = of_cores(jnp.concatenate([both[0, q:], both[1, q:]], axis=0))
    diag, lower, upper, rhs = after(diag, rhs, dot(ahead, lower), dot(behind, upper))

    solved = solve(of_cores(of_pair(diag)), (lower, rhs, upper))
    solved, lower, upper = lax.optimization_barrier((solved, lower, upper))
    forward, back = send(solved[q:], 4), send(solved[: q + g], -4)
    n = own[0].shape[0]
    at = lax.axis_index("far") * (4 * n)

    def rows_of(block):
        return lax.dynamic_slice_in_dim(block, at, 4 * n, axis=1)

    couplings = of_cores(of_pair(jnp.concatenate([rows_of(lower), rows_of(upper)], axis=1)))
    left = dot(forward, couplings[:, : 4 * n])
    right = dot(back, couplings[:, 4 * n :])
    new_diag = rows_of(diag).astype(jnp.float32) - left[g:] - right[:q]
    new_rhs = rows_of(rhs).astype(jnp.float32) - left[:g] - right[q:]
    done = jnp.concatenate([new_diag, new_rhs], axis=0).astype(jnp.bfloat16)
    done = lax.all_gather(done, "near", axis=0)
    done = jnp.where(near == 0, done[:, :, : 2 * n], done[:, :, 2 * n :])
    done = lax.all_gather(done, "c", axis=0)
    done = jnp.where(core == 0, done[..., :n], done[..., n:])
    out_diag = done[:, :, :q].reshape(m, n).T
    out_rhs = done[:, :, q:].reshape(r, n).T
    return out_diag[None], out_rhs[None]


def solution(mesh):
    finer = Mesh(mesh.devices.reshape(LAYERS, 4, 2, 2), AXES)
    placed = P("layer", ("far", "near", "c"), None)
    return jax.shard_map(
        on_device,
        mesh=finer,
        in_specs=(placed,) * 4,
        out_specs=(placed,) * 2,
        check_vma=False,
    )
```

time: 133 us -> 122 us (0.917)
  the two profiles are of different devices: /device:TPU:71 before, /device:TPU:193 now
where the time goes in v2:
time: 122 us; the launch traced here: 121 us
  blocking collectives  74.2 us (61%)
  starting transfers between devices  24.8 us (20%)
  waiting for transfers between devices  11.5 us (9%)
  Pallas kernels  4.55 us (4%)
  local copies, waits for them, and re-layouts  2.34 us (2%)
  matrix products  1.68 us (1%)
  other arithmetic  1.39 us (1%)
    all_to_all x1, blocking collectives, first_solve(): mine = lax.all_to_all(copies, ('far', 'near'), 0, 0, tiled=True)  29.7 us
    ppermute x6, starting transfers between devices, send(): return lax.ppermute(block, 'layer', pairs)  20.5 us
    all_gather x5, blocking collectives, of_cores(): return lax.all_gather(rows, 'c', axis=0, tiled=True)  16.7 us
    all_gather x3, blocking collectives, of_pair(): return lax.all_gather(rows, 'near', axis=0, tiled=True)  13.7 us
    ppermute x6, waiting for transfers between devices, send(): return lax.ppermute(block, 'layer', pairs)  9.64 us
    all_gather x1, blocking collectives, on_device(): lax.all_gather(jnp.concatenate([lower, upper], axis=0), 'near', axis=0)  7.54 us
    ppermute x1, starting transfers between devices, swap(): return lax.ppermute(block, 'c', [(0, 1), (1, 0)])  4.31 us
    all_gather x1, blocking collectives, on_device(): done = lax.all_gather(done, 'near', axis=0)  3.53 us
  transfers between devices with their start and end apart: 7, of which 3 were waited for; matrix products, arithmetic and copies ran while one was open for 1% of the time, Pallas kernels for 0%

profile of v2, /device:TPU:193, one launch (start us, length us, event | category | flops | bytes accessed | tf_op | source)
XLA Modules:
  0.0 121.5 jit_solution(8115111416782947899)
XLA Ops:
  1.5 29.7 %all_to_all.5.mine_ref = bf16[8,32,1664]{2,1,0:T(8,128)(2,1)S(1)} all-to-all(bf16[8,32,1664]{2,1,0:T(8,128)(2,1)S(1)} %broadcast_in_dim.12), channel_id=1, replica_groups=mesh['layer'=32,'far'=4,'near'=2,'c'=2] {'far','near'}, dimensions={0} | all-to-all | bytes 1703936 | tf_op jit(solution)/shard_map/all_to_all | solution.py:118
  31.2 4.3 %collective-permute-start = (bf16[8,32,1664]{2,1,0:T(8,128)(2,1)S(1)}, bf16[8,32,1664]{2,1,0:T(8,128)(2,1)S(1)}, u32[]{:S(2)}, u32[]{:S(2)}) collective-permute-start(bf16[8,32,1664]{2,1,0:T(8,128)(2,1)S(1)} %all_to_all.5.mine_ref), channel_id=1, source_target_pairs={{0,1},{1,0},{2,3},{3,2},{4,5},{5,4},{6,7},{7,6},{8,9},{9,8},{10,11... | collective-permute-start | bytes 2555912 | tf_op jit(solution)/shard_map/ppermute | solution.py:19
  35.6 1.9 %collective-permute-done.other_ref = bf16[8,32,1664]{2,1,0:T(8,128)(2,1)S(1)} collective-permute-done((bf16[8,32,1664]{2,1,0:T(8,128)(2,1)S(1)}, bf16[8,32,1664]{2,1,0:T(8,128)(2,1)S(1)}, u32[]{:S(2)}, u32[]{:S(2)}) %collective-permute-start) | collective-permute-done | bytes 852000 | tf_op jit(solution)/shard_map/ppermute | solution.py:19
  37.5 2.2 %shard_map.59 = (bf16[288,512]{1,0:T(8,128)(2,1)S(1)}, bf16[512,512]{1,0:T(8,128)(2,1)S(1)}, bf16[512,512]{1,0:T(8,128)(2,1)S(1)}, bf16[128,512]{1,0:T(8,128)(2,1)S(1)}, bf16[32,512]{1,0:T(8,128)(2,1)S(1)}) custom-call(s32[2]{0:T(128)S(1)} %pad_add_fusion.core_ref, bf16[8,32,1664]{2,1,0:T(8,128)(2,1)S(1)} %all_to_all.5.mine_ref, ...), custom_call_target="tpu_custom_call" | custom-call | flops 939524096 | bytes 4194304 | tf_op jit(solution)/shard_map/pallas_call | solution.py:122
  39.7 3.5 %collective-permute-start.2 = (bf16[288,512]{1,0:T(8,128)(2,1)S(1)}, bf16[288,512]{1,0:T(8,128)(2,1)S(1)}, u32[]{:S(2)}, u32[]{:S(2)}) collective-permute-start(bf16[288,512]{1,0:T(8,128)(2,1)S(1)} %get-tuple-element.14), channel_id=1, source_target_pairs={{16,0},{32,16},{48,32},{64,48},{80,64},{96,80},{112,96},{128,112},... | collective-permute-start | bytes 884744 | tf_op jit(solution)/shard_map/ppermute | solution.py:15
  43.2 1.9 %collective-permute-start.1 = (bf16[288,512]{1,0:T(8,128)(2,1)S(1)}, bf16[288,512]{1,0:T(8,128)(2,1)S(1)}, u32[]{:S(2)}, u32[]{:S(2)}) collective-permute-start(bf16[288,512]{1,0:T(8,128)(2,1)S(1)} %get-tuple-element.14), channel_id=1, source_target_pairs={{0,16},{16,32},{32,48},{48,64},{64,80},{80,96},{96,112},{112,128},... | collective-permute-start | bytes 884744 | tf_op jit(solution)/shard_map/ppermute | solution.py:15
  45.1 4.7 %collective-permute-done.2 = bf16[288,512]{1,0:T(8,128)(2,1)S(1)} collective-permute-done((bf16[288,512]{1,0:T(8,128)(2,1)S(1)}, bf16[288,512]{1,0:T(8,128)(2,1)S(1)}, u32[]{:S(2)}, u32[]{:S(2)}) %collective-permute-start.2) | collective-permute-done | bytes 294944 | tf_op jit(solution)/shard_map/ppermute | solution.py:15
  50.1 4.9 %collective-permute-done.1 = bf16[288,512]{1,0:T(8,128)(2,1)S(1)} collective-permute-done((bf16[288,512]{1,0:T(8,128)(2,1)S(1)}, bf16[288,512]{1,0:T(8,128)(2,1)S(1)}, u32[]{:S(2)}, u32[]{:S(2)}) %collective-permute-start.1) | collective-permute-done | bytes 294944 | tf_op jit(solution)/shard_map/ppermute | solution.py:15
  55.6 4.5 %all_gather.40 = bf16[256,512]{1,0:T(8,128)(2,1)S(1)} all-gather(bf16[128,512]{1,0:T(8,128)(2,1)S(1)} %get-tuple-element.28), channel_id=1, replica_groups=mesh['layer'=32,'far'=4,'near'=2,'c'=2] {'near'}, dimensions={0}, use_global_device_ids=true | all-gather | bytes 393216 | tf_op jit(solution)/shard_map/all_gather | solution.py:27
  60.1 4.5 %all_gather.41.diag_ref = bf16[512,512]{1,0:T(8,128)(2,1)S(1)} all-gather(bf16[256,512]{1,0:T(8,128)(2,1)S(1)} %all_gather.40), channel_id=1, replica_groups=mesh['layer'=32,'far'=4,'near'=2,'c'=2] {'c'}, dimensions={0}, use_global_device_ids=true | all-gather | bytes 786432 | tf_op jit(solution)/shard_map/all_gather | solution.py:23
  65.7 1.9 %collective-permute-start.4 = (bf16[288,512]{1,0:T(8,128)(2,1)S(1)}, bf16[288,512]{1,0:T(8,128)(2,1)S(1)}, u32[]{:S(2)}, u32[]{:S(2)}) collective-permute-start(bf16[288,512]{1,0:T(8,128)(2,1)S(1)} %shard_map.60), channel_id=1, source_target_pairs={{32,0},{48,16},{64,32},{80,48},{96,64},{112,80},{128,96},{144,112}... | collective-permute-start | bytes 884744 | tf_op jit(solution)/shard_map/ppermute | solution.py:15
  67.7 4.9 %collective-permute-start.3 = (bf16[288,512]{1,0:T(8,128)(2,1)S(1)}, bf16[288,512]{1,0:T(8,128)(2,1)S(1)}, u32[]{:S(2)}, u32[]{:S(2)}) collective-permute-start(bf16[288,512]{1,0:T(8,128)(2,1)S(1)} %shard_map.60), channel_id=1, source_target_pairs={{0,32},{16,48},{32,64},{48,80},{64,96},{80,112},{96,128},{112,144}... | collective-permute-start | bytes 884744 | tf_op jit(solution)/shard_map/ppermute | solution.py:15
  72.6 7.5 %all-gather = bf16[512,512]{1,0:T(8,128)(2,1)S(1)} all-gather(bf16[256,512]{1,0:T(8,128)(2,1)S(1)} %pad_maximum_fusion), channel_id=2, replica_groups=mesh['layer'=32,'far'=4,'near'=2,'c'=2] {'near'}, dimensions={0}, use_global_device_ids=true | all-gather | bytes 786432 | tf_op jit(solution)/shard_map/all_gather | solution.py:146
  80.2 3.7 %all_gather.44 = bf16[512,512]{1,0:T(8,128)(2,1)S(1)} all-gather(bf16[256,512]{1,0:T(8,128)(2,1)S(1)} %pad_maximum_fusion.1), channel_id=1, replica_groups=mesh['layer'=32,'far'=4,'near'=2,'c'=2] {'c'}, dimensions={0}, use_global_device_ids=true | all-gather | bytes 786432 | tf_op jit(solution)/shard_map/all_gather | solution.py:23
  83.9 2.2 %all_gather.45 = bf16[512,512]{1,0:T(8,128)(2,1)S(1)} all-gather(bf16[256,512]{1,0:T(8,128)(2,1)S(1)} %pad_maximum_fusion.2), channel_id=1, replica_groups=mesh['layer'=32,'far'=4,'near'=2,'c'=2] {'c'}, dimensions={0}, use_global_device_ids=true | all-gather | bytes 786432 | tf_op jit(solution)/shard_map/all_gather | solution.py:23
  86.8 5.4 %all_gather.46 = bf16[256,512]{1,0:T(8,128)(2,1)S(1)} all-gather(bf16[128,512]{1,0:T(8,128)(2,1)S(1)} %get-tuple-element.25), channel_id=1, replica_groups=mesh['layer'=32,'far'=4,'near'=2,'c'=2] {'near'}, dimensions={0}, use_global_device_ids=true | all-gather | bytes 393216 | tf_op jit(solution)/shard_map/all_gather | solution.py:27
  92.2 3.0 %all_gather.47.diag_ref = bf16[512,512]{1,0:T(8,128)(2,1)S(1)} all-gather(bf16[256,512]{1,0:T(8,128)(2,1)S(1)} %all_gather.46), channel_id=1, replica_groups=mesh['layer'=32,'far'=4,'near'=2,'c'=2] {'c'}, dimensions={0}, use_global_device_ids=true | all-gather | bytes 786432 | tf_op jit(solution)/shard_map/all_gather | solution.py:23
  95.2 1.2 shard_map.61
  96.5 6.4 %collective-permute-start.5 = (bf16[160,512]{1,0:T(8,128)(2,1)S(1)}, bf16[160,512]{1,0:T(8,128)(2,1)S(1)}, u32[]{:S(2)}, u32[]{:S(2)}) collective-permute-start(bf16[160,512]{1,0:T(8,128)(2,1)S(1)} %get-tuple-element.34), channel_id=1, source_target_pairs={{0,64},{16,80},{32,96},{48,112},{64,128},{80,144},{96,160},{112,17... | collective-permute-start | bytes 491528 | tf_op jit(solution)/shard_map/ppermute | solution.py:15
  102.9 1.9 %collective-permute-start.6 = (bf16[160,512]{1,0:T(8,128)(2,1)S(1)}, bf16[160,512]{1,0:T(8,128)(2,1)S(1)}, u32[]{:S(2)}, u32[]{:S(2)}) collective-permute-start(bf16[160,512]{1,0:T(8,128)(2,1)S(1)} %get-tuple-element.35), channel_id=1, source_target_pairs={{64,0},{80,16},{96,32},{112,48},{128,64},{144,80},{160,96},{176,11... | collective-permute-start | bytes 491528 | tf_op jit(solution)/shard_map/ppermute | solution.py:15
  104.8 3.8 %all_gather.48 = bf16[256,256]{1,0:T(8,128)(2,1)S(1)} all-gather(bf16[128,256]{1,0:T(8,128)(2,1)S(1)} %pad_maximum_fusion.4), channel_id=1, replica_groups=mesh['layer'=32,'far'=4,'near'=2,'c'=2] {'near'}, dimensions={0}, use_global_device_ids=true | all-gather | bytes 196608 | tf_op jit(solution)/shard_map/all_gather | solution.py:27
  108.6 3.4 %all_gather.49 = bf16[512,256]{1,0:T(8,128)(2,1)S(1)} all-gather(bf16[256,256]{1,0:T(8,128)(2,1)S(1)} %all_gather.48), channel_id=1, replica_groups=mesh['layer'=32,'far'=4,'near'=2,'c'=2] {'c'}, dimensions={0}, use_global_device_ids=true | all-gather | bytes 393216 | tf_op jit(solution)/shard_map/all_gather | solution.py:23
  112.5 3.5 %all_gather.50 = bf16[2,160,128]{2,1,0:T(8,128)(2,1)S(1)} all-gather(bf16[1,160,128]{2,1,0:T(8,128)(2,1)S(1)} %pad_maximum_fusion.5), channel_id=1, replica_groups=mesh['layer'=32,'far'=4,'near'=2,'c'=2] {'near'}, dimensions={0}, use_global_device_ids=true | all-gather | bytes 122880 | tf_op jit(solution)/shard_map/all_gather | solution.py:166
  116.3 3.1 %all-gather.1 = bf16[4,160,64]{1,2,0:T(8,128)(2,1)S(1)} all-gather(bf16[2,160,64]{1,2,0:T(8,128)(2,1)S(1)} %copy.8), channel_id=3, replica_groups=mesh['layer'=32,'far'=4,'near'=2,'c'=2] {'c'}, dimensions={0}, use_global_device_ids=true | all-gather | bytes 122880 | tf_op jit(solution)/shard_map/all_gather | solution.py:168
  (40 shorter events, 6.6 us)
Async XLA Ops:
  31.2 6.3 %collective-permute-start = (bf16[8,32,1664]{2,1,0:T(8,128)(2,1)S(1)}, bf16[8,32,1664]{2,1,0:T(8,128)(2,1)S(1)}, u32[]{:S(2)}, u32[]{:S(2)}) collective-permute-start(bf16[8,32,1664]{2,1,0:T(8,128)(2,1)S(1)} %all_to_all.5.mine_ref), channel_id=1, source_target_pairs={{0,1},{1,0},{2,3},{3,2},{4,5},{5,4},{6,7},{7,6},{8,9},{9,8},{10,11... | collective-permute-start | bytes 2555912 | tf_op jit(solution)/shard_map/ppermute | solution.py:19
  39.7 10.1 %collective-permute-start.2 = (bf16[288,512]{1,0:T(8,128)(2,1)S(1)}, bf16[288,512]{1,0:T(8,128)(2,1)S(1)}, u32[]{:S(2)}, u32[]{:S(2)}) collective-permute-start(bf16[288,512]{1,0:T(8,128)(2,1)S(1)} %get-tuple-element.14), channel_id=1, source_target_pairs={{16,0},{32,16},{48,32},{64,48},{80,64},{96,80},{112,96},{128,112},... | collective-permute-start | bytes 884744 | tf_op jit(solution)/shard_map/ppermute | solution.py:15
  43.2 11.9 %collective-permute-start.1 = (bf16[288,512]{1,0:T(8,128)(2,1)S(1)}, bf16[288,512]{1,0:T(8,128)(2,1)S(1)}, u32[]{:S(2)}, u32[]{:S(2)}) collective-permute-start(bf16[288,512]{1,0:T(8,128)(2,1)S(1)} %get-tuple-element.14), channel_id=1, source_target_pairs={{0,16},{16,32},{32,48},{48,64},{64,80},{80,96},{96,112},{112,128},... | collective-permute-start | bytes 884744 | tf_op jit(solution)/shard_map/ppermute | solution.py:15
  65.7 20.3 %collective-permute-start.4 = (bf16[288,512]{1,0:T(8,128)(2,1)S(1)}, bf16[288,512]{1,0:T(8,128)(2,1)S(1)}, u32[]{:S(2)}, u32[]{:S(2)}) collective-permute-start(bf16[288,512]{1,0:T(8,128)(2,1)S(1)} %shard_map.60), channel_id=1, source_target_pairs={{32,0},{48,16},{64,32},{80,48},{96,64},{112,80},{128,96},{144,112}... | collective-permute-start | bytes 884744 | tf_op jit(solution)/shard_map/ppermute | solution.py:15
  67.7 18.7 %collective-permute-start.3 = (bf16[288,512]{1,0:T(8,128)(2,1)S(1)}, bf16[288,512]{1,0:T(8,128)(2,1)S(1)}, u32[]{:S(2)}, u32[]{:S(2)}) collective-permute-start(bf16[288,512]{1,0:T(8,128)(2,1)S(1)} %shard_map.60), channel_id=1, source_target_pairs={{0,32},{16,48},{32,64},{48,80},{64,96},{80,112},{96,128},{112,144}... | collective-permute-start | bytes 884744 | tf_op jit(solution)/shard_map/ppermute | solution.py:15
  96.5 15.6 %collective-permute-start.5 = (bf16[160,512]{1,0:T(8,128)(2,1)S(1)}, bf16[160,512]{1,0:T(8,128)(2,1)S(1)}, u32[]{:S(2)}, u32[]{:S(2)}) collective-permute-start(bf16[160,512]{1,0:T(8,128)(2,1)S(1)} %get-tuple-element.34), channel_id=1, source_target_pairs={{0,64},{16,80},{32,96},{48,112},{64,128},{80,144},{96,160},{112,17... | collective-permute-start | bytes 491528 | tf_op jit(solution)/shard_map/ppermute | solution.py:15
  102.9 9.4 %collective-permute-start.6 = (bf16[160,512]{1,0:T(8,128)(2,1)S(1)}, bf16[160,512]{1,0:T(8,128)(2,1)S(1)}, u32[]{:S(2)}, u32[]{:S(2)}) collective-permute-start(bf16[160,512]{1,0:T(8,128)(2,1)S(1)} %get-tuple-element.35), channel_id=1, source_target_pairs={{64,0},{80,16},{96,32},{112,48},{128,64},{144,80},{160,96},{176,11... | collective-permute-start | bytes 491528 | tf_op jit(solution)/shard_map/ppermute | solution.py:15
  119.3 0.6 copy-start
  120.0 0.8 slice-start

commit v3 on v2

--- a/solution.py
+++ b/solution.py
@@ -70,6 +70,33 @@
         compiler_params=pltpu.CompilerParams(vmem_limit_bytes=24 * 2**20),
         cost_estimate=pl.CostEstimate(flops=2 * m * m * (2 * m + rows), bytes_accessed=4 * m * (m + rows), transcendentals=0),
     )(diag, *parts)
+
+
+def finish_kernel(core_ref, done_ref, diag_ref, rhs_ref):
+    n = diag_ref.shape[1]
+    q, g = diag_ref.shape[2] // 4, rhs_ref.shape[2] // 4
+    for own in range(2):
+
+        @pl.when(core_ref[0] == own)
+        def _(own=own):
+            for k in range(4):
+                turned = done_ref[k // 2, k % 2].astype(jnp.float32).T
+                turned = turned[own * n : own * n + n].astype(jnp.bfloat16)
+                diag_ref[0, :, k * q : k * q + q] = turned[:, :q]
+                rhs_ref[0, :, k * g : k * g + g] = turned[:, q:]
+
+
+def finish(done, core, n, m, r):
+    whole = pl.BlockSpec(memory_space=pltpu.VMEM)
+    shapes = ((1, n, m), (1, n, r))
+    return pl.pallas_call(
+        finish_kernel,
+        out_shape=tuple(jax.ShapeDtypeStruct(s, jnp.bfloat16) for s in shapes),
+        in_specs=[pl.BlockSpec(memory_space=pltpu.SMEM), whole],
+        out_specs=(whole, whole),
+        compiler_params=pltpu.CompilerParams(vmem_limit_bytes=8 * 2**20),
+        cost_estimate=pl.CostEstimate(flops=m * n, bytes_accessed=4 * m * n, transcendentals=0),
+    )(core.reshape(1).astype(jnp.int32), done)
 
 
 def after(diag, rhs, left, right):
@@ -166,10 +193,7 @@
     done = lax.all_gather(done, "near", axis=0)
     done = jnp.where(near == 0, done[:, :, : 2 * n], done[:, :, 2 * n :])
     done = lax.all_gather(done, "c", axis=0)
-    done = jnp.where(core == 0, done[..., :n], done[..., n:])
-    out_diag = done[:, :, :q].reshape(m, n).T
-    out_rhs = done[:, :, q:].reshape(r, n).T
-    return out_diag[None], out_rhs[None]
+    return finish(done, core, n, m, r)
 
 
 def solution(mesh):

time: 122 us -> 121 us (level)
  local copies, waits for them, and re-layouts: 2.34 us -> 0.39 us
    reshape x2 -> x0, local copies, waits for them, and re-layouts: 1.32 us -> none  [the longest x1 0.69 us: on_device(): out_rhs = done[:, :, q:].reshape(r, n).T]
where the time goes in v3:
time: 121 us; the launch traced here: 120 us
  blocking collectives  74.2 us (61%)
  starting transfers between devices  24.8 us (20%)
  waiting for transfers between devices  11.5 us (10%)
  Pallas kernels  5.38 us (4%)
  matrix products  1.68 us (1%)
  other arithmetic  1.39 us (1%)
    all_to_all x1, blocking collectives, first_solve(): mine = lax.all_to_all(copies, ('far', 'near'), 0, 0, tiled=True)  29.7 us
    ppermute x6, starting transfers between devices, send(): return lax.ppermute(block, 'layer', pairs)  20.5 us
    all_gather x5, blocking collectives, of_cores(): return lax.all_gather(rows, 'c', axis=0, tiled=True)  16.7 us
    all_gather x3, blocking collectives, of_pair(): return lax.all_gather(rows, 'near', axis=0, tiled=True)  13.7 us
    ppermute x6, waiting for transfers between devices, send(): return lax.ppermute(block, 'layer', pairs)  9.64 us
    all_gather x1, blocking collectives, on_device(): lax.all_gather(jnp.concatenate([lower, upper], axis=0), 'near', axis=0)  7.57 us
    ppermute x1, starting transfers between devices, swap(): return lax.ppermute(block, 'c', [(0, 1), (1, 0)])  4.31 us
    all_gather x1, blocking collectives, on_device(): done = lax.all_gather(done, 'near', axis=0)  3.53 us
  transfers between devices with their start and end apart: 7, of which 3 were waited for; matrix products, arithmetic and copies ran while one was open for 1% of the time, Pallas kernels for 0%

profile of v3, /device:TPU:193, one launch (start us, length us, event | category | flops | bytes accessed | tf_op | source)
XLA Modules:
  0.0 120.3 jit_solution(12050071489659891331)
XLA Ops:
  1.5 29.7 %all_to_all.5.mine_ref = bf16[8,32,1664]{2,1,0:T(8,128)(2,1)S(1)} all-to-all(bf16[8,32,1664]{2,1,0:T(8,128)(2,1)S(1)} %broadcast_in_dim.2), channel_id=1, replica_groups=mesh['layer'=32,'far'=4,'near'=2,'c'=2] {'far','near'}, dimensions={0} | all-to-all | bytes 1703936 | tf_op jit(solution)/shard_map/all_to_all | solution.py:145
  31.2 4.3 %collective-permute-start = (bf16[8,32,1664]{2,1,0:T(8,128)(2,1)S(1)}, bf16[8,32,1664]{2,1,0:T(8,128)(2,1)S(1)}, u32[]{:S(2)}, u32[]{:S(2)}) collective-permute-start(bf16[8,32,1664]{2,1,0:T(8,128)(2,1)S(1)} %all_to_all.5.mine_ref), channel_id=1, source_target_pairs={{0,1},{1,0},{2,3},{3,2},{4,5},{5,4},{6,7},{7,6},{8,9},{9,8},{10,11... | collective-permute-start | bytes 2555912 | tf_op jit(solution)/shard_map/ppermute | solution.py:19
  35.6 1.9 %collective-permute-done.other_ref = bf16[8,32,1664]{2,1,0:T(8,128)(2,1)S(1)} collective-permute-done((bf16[8,32,1664]{2,1,0:T(8,128)(2,1)S(1)}, bf16[8,32,1664]{2,1,0:T(8,128)(2,1)S(1)}, u32[]{:S(2)}, u32[]{:S(2)}) %collective-permute-start) | collective-permute-done | bytes 852000 | tf_op jit(solution)/shard_map/ppermute | solution.py:19
  37.5 2.2 %shard_map.59 = (bf16[288,512]{1,0:T(8,128)(2,1)S(1)}, bf16[512,512]{1,0:T(8,128)(2,1)S(1)}, bf16[512,512]{1,0:T(8,128)(2,1)S(1)}, bf16[128,512]{1,0:T(8,128)(2,1)S(1)}, bf16[32,512]{1,0:T(8,128)(2,1)S(1)}) custom-call(s32[2]{0:T(128)S(1)} %pad_add_fusion.core_ref, bf16[8,32,1664]{2,1,0:T(8,128)(2,1)S(1)} %all_to_all.5.mine_ref, ...), custom_call_target="tpu_custom_call" | custom-call | flops 939524096 | bytes 4194304 | tf_op jit(solution)/shard_map/pallas_call | solution.py:149
  39.7 3.5 %collective-permute-start.2 = (bf16[288,512]{1,0:T(8,128)(2,1)S(1)}, bf16[288,512]{1,0:T(8,128)(2,1)S(1)}, u32[]{:S(2)}, u32[]{:S(2)}) collective-permute-start(bf16[288,512]{1,0:T(8,128)(2,1)S(1)} %get-tuple-element.14), channel_id=1, source_target_pairs={{16,0},{32,16},{48,32},{64,48},{80,64},{96,80},{112,96},{128,112},... | collective-permute-start | bytes 884744 | tf_op jit(solution)/shard_map/ppermute | solution.py:15
  43.2 1.9 %collective-permute-start.1 = (bf16[288,512]{1,0:T(8,128)(2,1)S(1)}, bf16[288,512]{1,0:T(8,128)(2,1)S(1)}, u32[]{:S(2)}, u32[]{:S(2)}) collective-permute-start(bf16[288,512]{1,0:T(8,128)(2,1)S(1)} %get-tuple-element.14), channel_id=1, source_target_pairs={{0,16},{16,32},{32,48},{48,64},{64,80},{80,96},{96,112},{112,128},... | collective-permute-start | bytes 884744 | tf_op jit(solution)/shard_map/ppermute | solution.py:15
  45.1 4.7 %collective-permute-done.2 = bf16[288,512]{1,0:T(8,128)(2,1)S(1)} collective-permute-done((bf16[288,512]{1,0:T(8,128)(2,1)S(1)}, bf16[288,512]{1,0:T(8,128)(2,1)S(1)}, u32[]{:S(2)}, u32[]{:S(2)}) %collective-permute-start.2) | collective-permute-done | bytes 294944 | tf_op jit(solution)/shard_map/ppermute | solution.py:15
  50.2 4.9 %collective-permute-done.1 = bf16[288,512]{1,0:T(8,128)(2,1)S(1)} collective-permute-done((bf16[288,512]{1,0:T(8,128)(2,1)S(1)}, bf16[288,512]{1,0:T(8,128)(2,1)S(1)}, u32[]{:S(2)}, u32[]{:S(2)}) %collective-permute-start.1) | collective-permute-done | bytes 294944 | tf_op jit(solution)/shard_map/ppermute | solution.py:15
  55.6 4.5 %all_gather.40 = bf16[256,512]{1,0:T(8,128)(2,1)S(1)} all-gather(bf16[128,512]{1,0:T(8,128)(2,1)S(1)} %get-tuple-element.28), channel_id=1, replica_groups=mesh['layer'=32,'far'=4,'near'=2,'c'=2] {'near'}, dimensions={0}, use_global_device_ids=true | all-gather | bytes 393216 | tf_op jit(solution)/shard_map/all_gather | solution.py:27
  60.1 4.5 %all_gather.41.diag_ref = bf16[512,512]{1,0:T(8,128)(2,1)S(1)} all-gather(bf16[256,512]{1,0:T(8,128)(2,1)S(1)} %all_gather.40), channel_id=1, replica_groups=mesh['layer'=32,'far'=4,'near'=2,'c'=2] {'c'}, dimensions={0}, use_global_device_ids=true | all-gather | bytes 786432 | tf_op jit(solution)/shard_map/all_gather | solution.py:23
  64.5 1.2 shard_map.60
  65.7 1.9 %collective-permute-start.4 = (bf16[288,512]{1,0:T(8,128)(2,1)S(1)}, bf16[288,512]{1,0:T(8,128)(2,1)S(1)}, u32[]{:S(2)}, u32[]{:S(2)}) collective-permute-start(bf16[288,512]{1,0:T(8,128)(2,1)S(1)} %shard_map.60), channel_id=1, source_target_pairs={{32,0},{48,16},{64,32},{80,48},{96,64},{112,80},{128,96},{144,112}... | collective-permute-start | bytes 884744 | tf_op jit(solution)/shard_map/ppermute | solution.py:15
  67.7 4.9 %collective-permute-start.3 = (bf16[288,512]{1,0:T(8,128)(2,1)S(1)}, bf16[288,512]{1,0:T(8,128)(2,1)S(1)}, u32[]{:S(2)}, u32[]{:S(2)}) collective-permute-start(bf16[288,512]{1,0:T(8,128)(2,1)S(1)} %shard_map.60), channel_id=1, source_target_pairs={{0,32},{16,48},{32,64},{48,80},{64,96},{80,112},{96,128},{112,144}... | collective-permute-start | bytes 884744 | tf_op jit(solution)/shard_map/ppermute | solution.py:15
  72.6 7.6 %all-gather = bf16[512,512]{1,0:T(8,128)(2,1)S(1)} all-gather(bf16[256,512]{1,0:T(8,128)(2,1)S(1)} %pad_maximum_fusion), channel_id=2, replica_groups=mesh['layer'=32,'far'=4,'near'=2,'c'=2] {'near'}, dimensions={0}, use_global_device_ids=true | all-gather | bytes 786432 | tf_op jit(solution)/shard_map/all_gather | solution.py:173
  80.2 3.6 %all_gather.44 = bf16[512,512]{1,0:T(8,128)(2,1)S(1)} all-gather(bf16[256,512]{1,0:T(8,128)(2,1)S(1)} %pad_maximum_fusion.1), channel_id=1, replica_groups=mesh['layer'=32,'far'=4,'near'=2,'c'=2] {'c'}, dimensions={0}, use_global_device_ids=true | all-gather | bytes 786432 | tf_op jit(solution)/shard_map/all_gather | solution.py:23
  83.9 2.2 %all_gather.45 = bf16[512,512]{1,0:T(8,128)(2,1)S(1)} all-gather(bf16[256,512]{1,0:T(8,128)(2,1)S(1)} %pad_maximum_fusion.2), channel_id=1, replica_groups=mesh['layer'=32,'far'=4,'near'=2,'c'=2] {'c'}, dimensions={0}, use_global_device_ids=true | all-gather | bytes 786432 | tf_op jit(solution)/shard_map/all_gather | solution.py:23
  86.8 5.4 %all_gather.46 = bf16[256,512]{1,0:T(8,128)(2,1)S(1)} all-gather(bf16[128,512]{1,0:T(8,128)(2,1)S(1)} %get-tuple-element.25), channel_id=1, replica_groups=mesh['layer'=32,'far'=4,'near'=2,'c'=2] {'near'}, dimensions={0}, use_global_device_ids=true | all-gather | bytes 393216 | tf_op jit(solution)/shard_map/all_gather | solution.py:27
  92.2 3.0 %all_gather.47.diag_ref = bf16[512,512]{1,0:T(8,128)(2,1)S(1)} all-gather(bf16[256,512]{1,0:T(8,128)(2,1)S(1)} %all_gather.46), channel_id=1, replica_groups=mesh['layer'=32,'far'=4,'near'=2,'c'=2] {'c'}, dimensions={0}, use_global_device_ids=true | all-gather | bytes 786432 | tf_op jit(solution)/shard_map/all_gather | solution.py:23
  96.4 6.4 %collective-permute-start.5 = (bf16[160,512]{1,0:T(8,128)(2,1)S(1)}, bf16[160,512]{1,0:T(8,128)(2,1)S(1)}, u32[]{:S(2)}, u32[]{:S(2)}) collective-permute-start(bf16[160,512]{1,0:T(8,128)(2,1)S(1)} %get-tuple-element.34), channel_id=1, source_target_pairs={{0,64},{16,80},{32,96},{48,112},{64,128},{80,144},{96,160},{112,17... | collective-permute-start | bytes 491528 | tf_op jit(solution)/shard_map/ppermute | solution.py:15
  102.9 1.9 %collective-permute-start.6 = (bf16[160,512]{1,0:T(8,128)(2,1)S(1)}, bf16[160,512]{1,0:T(8,128)(2,1)S(1)}, u32[]{:S(2)}, u32[]{:S(2)}) collective-permute-start(bf16[160,512]{1,0:T(8,128)(2,1)S(1)} %get-tuple-element.35), channel_id=1, source_target_pairs={{64,0},{80,16},{96,32},{112,48},{128,64},{144,80},{160,96},{176,11... | collective-permute-start | bytes 491528 | tf_op jit(solution)/shard_map/ppermute | solution.py:15
  104.8 3.8 %all_gather.48 = bf16[256,256]{1,0:T(8,128)(2,1)S(1)} all-gather(bf16[128,256]{1,0:T(8,128)(2,1)S(1)} %pad_maximum_fusion.4), channel_id=1, replica_groups=mesh['layer'=32,'far'=4,'near'=2,'c'=2] {'near'}, dimensions={0}, use_global_device_ids=true | all-gather | bytes 196608 | tf_op jit(solution)/shard_map/all_gather | solution.py:27
  108.6 3.4 %all_gather.49 = bf16[512,256]{1,0:T(8,128)(2,1)S(1)} all-gather(bf16[256,256]{1,0:T(8,128)(2,1)S(1)} %all_gather.48), channel_id=1, replica_groups=mesh['layer'=32,'far'=4,'near'=2,'c'=2] {'c'}, dimensions={0}, use_global_device_ids=true | all-gather | bytes 393216 | tf_op jit(solution)/shard_map/all_gather | solution.py:23
  112.5 3.5 %all_gather.50 = bf16[2,160,128]{2,1,0:T(8,128)(2,1)S(1)} all-gather(bf16[1,160,128]{2,1,0:T(8,128)(2,1)S(1)} %pad_maximum_fusion.5), channel_id=1, replica_groups=mesh['layer'=32,'far'=4,'near'=2,'c'=2] {'near'}, dimensions={0}, use_global_device_ids=true | all-gather | bytes 122880 | tf_op jit(solution)/shard_map/all_gather | solution.py:193
  116.3 3.1 %all-gather.1 = bf16[4,160,64]{1,2,0:T(8,128)(2,1)S(1)} all-gather(bf16[2,160,64]{1,2,0:T(8,128)(2,1)S(1)} %copy.6), channel_id=3, replica_groups=mesh['layer'=32,'far'=4,'near'=2,'c'=2] {'c'}, dimensions={0}, use_global_device_ids=true | all-gather | bytes 122880 | tf_op jit(solution)/shard_map/all_gather | solution.py:195
  (32 shorter events, 5.5 us)
Async XLA Ops:
  31.2 6.3 %collective-permute-start = (bf16[8,32,1664]{2,1,0:T(8,128)(2,1)S(1)}, bf16[8,32,1664]{2,1,0:T(8,128)(2,1)S(1)}, u32[]{:S(2)}, u32[]{:S(2)}) collective-permute-start(bf16[8,32,1664]{2,1,0:T(8,128)(2,1)S(1)} %all_to_all.5.mine_ref), channel_id=1, source_target_pairs={{0,1},{1,0},{2,3},{3,2},{4,5},{5,4},{6,7},{7,6},{8,9},{9,8},{10,11... | collective-permute-start | bytes 2555912 | tf_op jit(solution)/shard_map/ppermute | solution.py:19
  39.7 10.1 %collective-permute-start.2 = (bf16[288,512]{1,0:T(8,128)(2,1)S(1)}, bf16[288,512]{1,0:T(8,128)(2,1)S(1)}, u32[]{:S(2)}, u32[]{:S(2)}) collective-permute-start(bf16[288,512]{1,0:T(8,128)(2,1)S(1)} %get-tuple-element.14), channel_id=1, source_target_pairs={{16,0},{32,16},{48,32},{64,48},{80,64},{96,80},{112,96},{128,112},... | collective-permute-start | bytes 884744 | tf_op jit(solution)/shard_map/ppermute | solution.py:15
  43.2 11.9 %collective-permute-start.1 = (bf16[288,512]{1,0:T(8,128)(2,1)S(1)}, bf16[288,512]{1,0:T(8,128)(2,1)S(1)}, u32[]{:S(2)}, u32[]{:S(2)}) collective-permute-start(bf16[288,512]{1,0:T(8,128)(2,1)S(1)} %get-tuple-element.14), channel_id=1, source_target_pairs={{0,16},{16,32},{32,48},{48,64},{64,80},{80,96},{96,112},{112,128},... | collective-permute-start | bytes 884744 | tf_op jit(solution)/shard_map/ppermute | solution.py:15
  65.7 20.3 %collective-permute-start.4 = (bf16[288,512]{1,0:T(8,128)(2,1)S(1)}, bf16[288,512]{1,0:T(8,128)(2,1)S(1)}, u32[]{:S(2)}, u32[]{:S(2)}) collective-permute-start(bf16[288,512]{1,0:T(8,128)(2,1)S(1)} %shard_map.60), channel_id=1, source_target_pairs={{32,0},{48,16},{64,32},{80,48},{96,64},{112,80},{128,96},{144,112}... | collective-permute-start | bytes 884744 | tf_op jit(solution)/shard_map/ppermute | solution.py:15
  67.7 18.7 %collective-permute-start.3 = (bf16[288,512]{1,0:T(8,128)(2,1)S(1)}, bf16[288,512]{1,0:T(8,128)(2,1)S(1)}, u32[]{:S(2)}, u32[]{:S(2)}) collective-permute-start(bf16[288,512]{1,0:T(8,128)(2,1)S(1)} %shard_map.60), channel_id=1, source_target_pairs={{0,32},{16,48},{32,64},{48,80},{64,96},{80,112},{96,128},{112,144}... | collective-permute-start | bytes 884744 | tf_op jit(solution)/shard_map/ppermute | solution.py:15
  96.4 15.6 %collective-permute-start.5 = (bf16[160,512]{1,0:T(8,128)(2,1)S(1)}, bf16[160,512]{1,0:T(8,128)(2,1)S(1)}, u32[]{:S(2)}, u32[]{:S(2)}) collective-permute-start(bf16[160,512]{1,0:T(8,128)(2,1)S(1)} %get-tuple-element.34), channel_id=1, source_target_pairs={{0,64},{16,80},{32,96},{48,112},{64,128},{80,144},{96,160},{112,17... | collective-permute-start | bytes 491528 | tf_op jit(solution)/shard_map/ppermute | solution.py:15
  102.9 9.4 %collective-permute-start.6 = (bf16[160,512]{1,0:T(8,128)(2,1)S(1)}, bf16[160,512]{1,0:T(8,128)(2,1)S(1)}, u32[]{:S(2)}, u32[]{:S(2)}) collective-permute-start(bf16[160,512]{1,0:T(8,128)(2,1)S(1)} %get-tuple-element.35), channel_id=1, source_target_pairs={{64,0},{80,16},{96,32},{112,48},{128,64},{144,80},{160,96},{176,11... | collective-permute-start | bytes 491528 | tf_op jit(solution)/shard_map/ppermute | solution.py:15

commit v4 on v3

--- a/solution.py
+++ b/solution.py
@@ -175,16 +175,17 @@
     upper = of_cores(jnp.concatenate([both[0, q:], both[1, q:]], axis=0))
     diag, lower, upper, rhs = after(diag, rhs, dot(ahead, lower), dot(behind, upper))
 
-    solved = solve(of_cores(of_pair(diag)), (lower, rhs, upper))
-    solved, lower, upper = lax.optimization_barrier((solved, lower, upper))
-    forward, back = send(solved[q:], 4), send(solved[: q + g], -4)
     n = own[0].shape[0]
     at = lax.axis_index("far") * (4 * n)
 
     def rows_of(block):
         return lax.dynamic_slice_in_dim(block, at, 4 * n, axis=1)
 
-    couplings = of_cores(of_pair(jnp.concatenate([rows_of(lower), rows_of(upper)], axis=1)))
+    wide = of_pair(jnp.concatenate([diag, rows_of(lower), rows_of(upper)], axis=1))
+    solved = solve(of_cores(wide[:, :m]), (lower, rhs, upper))
+    solved, couplings = lax.optimization_barrier((solved, wide[:, m:]))
+    forward, back = send(solved[q:], 4), send(solved[: q + g], -4)
+    couplings = of_cores(couplings)
     left = dot(forward, couplings[:, : 4 * n])
     right = dot(back, couplings[:, 4 * n :])
     new_diag = rows_of(diag).astype(jnp.float32) - left[g:] - right[:q]

time: 121 us -> 119 us (0.983)
  the two profiles are of different devices: /device:TPU:193 before, /device:TPU:257 now
where the time goes in v4:
time: 119 us; the launch traced here: 118 us
  blocking collectives  71.8 us (60%)
  starting transfers between devices  21.8 us (18%)
  waiting for transfers between devices  15.2 us (13%)
  Pallas kernels  5.38 us (5%)
  matrix products  1.68 us (1%)
  other arithmetic  1.39 us (1%)
    all_to_all x1, blocking collectives, first_solve(): mine = lax.all_to_all(copies, ('far', 'near'), 0, 0, tiled=True)  29.7 us
    ppermute x6, starting transfers between devices, send(): return lax.ppermute(block, 'layer', pairs)  17.5 us
    all_gather x5, blocking collectives, of_cores(): return lax.all_gather(rows, 'c', axis=0, tiled=True)  15.8 us
    ppermute x6, waiting for transfers between devices, send(): return lax.ppermute(block, 'layer', pairs)  13.3 us
    all_gather x2, blocking collectives, of_pair(): return lax.all_gather(rows, 'near', axis=0, tiled=True)  11.3 us
    all_gather x1, blocking collectives, on_device(): lax.all_gather(jnp.concatenate([lower, upper], axis=0), 'near', axis=0)  7.57 us
    ppermute x1, starting transfers between devices, swap(): return lax.ppermute(block, 'c', [(0, 1), (1, 0)])  4.31 us
    all_gather x1, blocking collectives, on_device(): done = lax.all_gather(done, 'c', axis=0)  3.89 us
  transfers between devices with their start and end apart: 7, of which 4 were waited for; matrix products, arithmetic and copies ran while one was open for 1% of the time, Pallas kernels for 0%

profile of v4, /device:TPU:257, one launch (start us, length us, event | category | flops | bytes accessed | tf_op | source)
XLA Modules:
  0.0 118.5 jit_solution(6402199574247236166)
XLA Ops:
  1.5 29.7 %all_to_all.5.mine_ref = bf16[8,32,1664]{2,1,0:T(8,128)(2,1)S(1)} all-to-all(bf16[8,32,1664]{2,1,0:T(8,128)(2,1)S(1)} %broadcast_in_dim.2), channel_id=1, replica_groups=mesh['layer'=32,'far'=4,'near'=2,'c'=2] {'far','near'}, dimensions={0} | all-to-all | bytes 1703936 | tf_op jit(solution)/shard_map/all_to_all | solution.py:145
  31.2 4.3 %collective-permute-start = (bf16[8,32,1664]{2,1,0:T(8,128)(2,1)S(1)}, bf16[8,32,1664]{2,1,0:T(8,128)(2,1)S(1)}, u32[]{:S(2)}, u32[]{:S(2)}) collective-permute-start(bf16[8,32,1664]{2,1,0:T(8,128)(2,1)S(1)} %all_to_all.5.mine_ref), channel_id=1, source_target_pairs={{0,1},{1,0},{2,3},{3,2},{4,5},{5,4},{6,7},{7,6},{8,9},{9,8},{10,11... | collective-permute-start | bytes 2555912 | tf_op jit(solution)/shard_map/ppermute | solution.py:19
  35.6 1.9 %collective-permute-done.other_ref = bf16[8,32,1664]{2,1,0:T(8,128)(2,1)S(1)} collective-permute-done((bf16[8,32,1664]{2,1,0:T(8,128)(2,1)S(1)}, bf16[8,32,1664]{2,1,0:T(8,128)(2,1)S(1)}, u32[]{:S(2)}, u32[]{:S(2)}) %collective-permute-start) | collective-permute-done | bytes 852000 | tf_op jit(solution)/shard_map/ppermute | solution.py:19
  37.5 2.2 %shard_map.59 = (bf16[288,512]{1,0:T(8,128)(2,1)S(1)}, bf16[512,512]{1,0:T(8,128)(2,1)S(1)}, bf16[512,512]{1,0:T(8,128)(2,1)S(1)}, bf16[128,512]{1,0:T(8,128)(2,1)S(1)}, bf16[32,512]{1,0:T(8,128)(2,1)S(1)}) custom-call(s32[2]{0:T(128)S(1)} %pad_add_fusion.core_ref, bf16[8,32,1664]{2,1,0:T(8,128)(2,1)S(1)} %all_to_all.5.mine_ref, ...), custom_call_target="tpu_custom_call" | custom-call | flops 939524096 | bytes 4194304 | tf_op jit(solution)/shard_map/pallas_call | solution.py:149
  39.7 3.5 %collective-permute-start.2 = (bf16[288,512]{1,0:T(8,128)(2,1)S(1)}, bf16[288,512]{1,0:T(8,128)(2,1)S(1)}, u32[]{:S(2)}, u32[]{:S(2)}) collective-permute-start(bf16[288,512]{1,0:T(8,128)(2,1)S(1)} %get-tuple-element.13), channel_id=1, source_target_pairs={{16,0},{32,16},{48,32},{64,48},{80,64},{96,80},{112,96},{128,112},... | collective-permute-start | bytes 884744 | tf_op jit(solution)/shard_map/ppermute | solution.py:15
  43.2 1.9 %collective-permute-start.1 = (bf16[288,512]{1,0:T(8,128)(2,1)S(1)}, bf16[288,512]{1,0:T(8,128)(2,1)S(1)}, u32[]{:S(2)}, u32[]{:S(2)}) collective-permute-start(bf16[288,512]{1,0:T(8,128)(2,1)S(1)} %get-tuple-element.13), channel_id=1, source_target_pairs={{0,16},{16,32},{32,48},{48,64},{64,80},{80,96},{96,112},{112,128},... | collective-permute-start | bytes 884744 | tf_op jit(solution)/shard_map/ppermute | solution.py:15
  45.1 4.7 %collective-permute-done.2 = bf16[288,512]{1,0:T(8,128)(2,1)S(1)} collective-permute-done((bf16[288,512]{1,0:T(8,128)(2,1)S(1)}, bf16[288,512]{1,0:T(8,128)(2,1)S(1)}, u32[]{:S(2)}, u32[]{:S(2)}) %collective-permute-start.2) | collective-permute-done | bytes 294944 | tf_op jit(solution)/shard_map/ppermute | solution.py:15
  50.1 6.1 %collective-permute-done.1 = bf16[288,512]{1,0:T(8,128)(2,1)S(1)} collective-permute-done((bf16[288,512]{1,0:T(8,128)(2,1)S(1)}, bf16[288,512]{1,0:T(8,128)(2,1)S(1)}, u32[]{:S(2)}, u32[]{:S(2)}) %collective-permute-start.1) | collective-permute-done | bytes 294944 | tf_op jit(solution)/shard_map/ppermute | solution.py:15
  56.8 4.5 %all_gather.37 = bf16[256,512]{1,0:T(8,128)(2,1)S(1)} all-gather(bf16[128,512]{1,0:T(8,128)(2,1)S(1)} %get-tuple-element.26), channel_id=1, replica_groups=mesh['layer'=32,'far'=4,'near'=2,'c'=2] {'near'}, dimensions={0}, use_global_device_ids=true | all-gather | bytes 393216 | tf_op jit(solution)/shard_map/all_gather | solution.py:27
  61.3 4.5 %all_gather.38.diag_ref = bf16[512,512]{1,0:T(8,128)(2,1)S(1)} all-gather(bf16[256,512]{1,0:T(8,128)(2,1)S(1)} %all_gather.37), channel_id=1, replica_groups=mesh['layer'=32,'far'=4,'near'=2,'c'=2] {'c'}, dimensions={0}, use_global_device_ids=true | all-gather | bytes 786432 | tf_op jit(solution)/shard_map/all_gather | solution.py:23
  65.7 1.2 %shard_map.60 = bf16[288,512]{1,0:T(8,128)(2,1)S(1)} custom-call(bf16[512,512]{1,0:T(8,128)(2,1)S(1)} %all_gather.38.diag_ref, bf16[128,512]{1,0:T(8,128)(2,1)S(1)} %get-tuple-element.18.refs_0_, bf16[32,512]{1,0:T(8,128)(2,1)S(1)} %fusion.12.refs_1_, bf16[128,512]{1,0:T(8,128)(2,1)S(1)} %get-tuple-element.19.refs_2_), custom_call_target="tpu_custom_call" | custom-call | flops 687865856 | bytes 1638400 | tf_op jit(solution)/shard_map/pallas_call | solution.py:65
  66.9 1.9 %collective-permute-start.4 = (bf16[288,512]{1,0:T(8,128)(2,1)S(1)}, bf16[288,512]{1,0:T(8,128)(2,1)S(1)}, u32[]{:S(2)}, u32[]{:S(2)}) collective-permute-start(bf16[288,512]{1,0:T(8,128)(2,1)S(1)} %shard_map.60), channel_id=1, source_target_pairs={{32,0},{48,16},{64,32},{80,48},{96,64},{112,80},{128,96},{144,112}... | collective-permute-start | bytes 884744 | tf_op jit(solution)/shard_map/ppermute | solution.py:15
  68.9 4.9 %collective-permute-start.3 = (bf16[288,512]{1,0:T(8,128)(2,1)S(1)}, bf16[288,512]{1,0:T(8,128)(2,1)S(1)}, u32[]{:S(2)}, u32[]{:S(2)}) collective-permute-start(bf16[288,512]{1,0:T(8,128)(2,1)S(1)} %shard_map.60), channel_id=1, source_target_pairs={{0,32},{16,48},{32,64},{48,80},{64,96},{80,112},{96,128},{112,144}... | collective-permute-start | bytes 884744 | tf_op jit(solution)/shard_map/ppermute | solution.py:15
  73.8 7.6 %all-gather = bf16[512,512]{1,0:T(8,128)(2,1)S(1)} all-gather(bf16[256,512]{1,0:T(8,128)(2,1)S(1)} %pad_maximum_fusion), channel_id=2, replica_groups=mesh['layer'=32,'far'=4,'near'=2,'c'=2] {'near'}, dimensions={0}, use_global_device_ids=true | all-gather | bytes 786432 | tf_op jit(solution)/shard_map/all_gather | solution.py:173
  81.4 3.6 %all_gather.41 = bf16[512,512]{1,0:T(8,128)(2,1)S(1)} all-gather(bf16[256,512]{1,0:T(8,128)(2,1)S(1)} %pad_maximum_fusion.1), channel_id=1, replica_groups=mesh['layer'=32,'far'=4,'near'=2,'c'=2] {'c'}, dimensions={0}, use_global_device_ids=true | all-gather | bytes 786432 | tf_op jit(solution)/shard_map/all_gather | solution.py:23
  85.1 2.2 %all_gather.42 = bf16[512,512]{1,0:T(8,128)(2,1)S(1)} all-gather(bf16[256,512]{1,0:T(8,128)(2,1)S(1)} %pad_maximum_fusion.2), channel_id=1, replica_groups=mesh['layer'=32,'far'=4,'near'=2,'c'=2] {'c'}, dimensions={0}, use_global_device_ids=true | all-gather | bytes 786432 | tf_op jit(solution)/shard_map/all_gather | solution.py:23
  88.1 6.8 %all_gather.43 = bf16[256,768]{1,0:T(8,128)(2,1)S(1)} all-gather(bf16[128,768]{1,0:T(8,128)(2,1)S(1)} %pad_maximum_fusion.3), channel_id=1, replica_groups=mesh['layer'=32,'far'=4,'near'=2,'c'=2] {'near'}, dimensions={0}, use_global_device_ids=true | all-gather | bytes 589824 | tf_op jit(solution)/shard_map/all_gather | solution.py:27
  94.9 3.0 %all_gather.44.diag_ref = bf16[512,512]{1,0:T(8,128)(2,1)S(1)} all-gather(bf16[256,512]{1,0:T(8,128)(2,1)S(1)} %slice.126), channel_id=1, replica_groups=mesh['layer'=32,'far'=4,'near'=2,'c'=2] {'c'}, dimensions={0}, use_global_device_ids=true | all-gather | bytes 786432 | tf_op jit(solution)/shard_map/all_gather | solution.py:23
  99.2 1.9 %collective-permute-start.6 = (bf16[160,512]{1,0:T(8,128)(2,1)S(1)}, bf16[160,512]{1,0:T(8,128)(2,1)S(1)}, u32[]{:S(2)}, u32[]{:S(2)}) collective-permute-start(bf16[160,512]{1,0:T(8,128)(2,1)S(1)} %get-tuple-element.33), channel_id=1, source_target_pairs={{64,0},{80,16},{96,32},{112,48},{128,64},{144,80},{160,96},{176,11... | collective-permute-start | bytes 491528 | tf_op jit(solution)/shard_map/ppermute | solution.py:15
  101.1 3.4 %collective-permute-start.5 = (bf16[160,512]{1,0:T(8,128)(2,1)S(1)}, bf16[160,512]{1,0:T(8,128)(2,1)S(1)}, u32[]{:S(2)}, u32[]{:S(2)}) collective-permute-start(bf16[160,512]{1,0:T(8,128)(2,1)S(1)} %get-tuple-element.32), channel_id=1, source_target_pairs={{0,64},{16,80},{32,96},{48,112},{64,128},{80,144},{96,160},{112,17... | collective-permute-start | bytes 491528 | tf_op jit(solution)/shard_map/ppermute | solution.py:15
  104.5 2.6 %all_gather.45 = bf16[512,256]{1,0:T(8,128)(2,1)S(1)} all-gather(bf16[256,256]{1,0:T(8,128)(2,1)S(1)} %slice.129), channel_id=1, replica_groups=mesh['layer'=32,'far'=4,'near'=2,'c'=2] {'c'}, dimensions={0}, use_global_device_ids=true | all-gather | bytes 393216 | tf_op jit(solution)/shard_map/all_gather | solution.py:23
  107.2 2.4 %collective-permute-done.5 = bf16[160,512]{1,0:T(8,128)(2,1)S(1)} collective-permute-done((bf16[160,512]{1,0:T(8,128)(2,1)S(1)}, bf16[160,512]{1,0:T(8,128)(2,1)S(1)}, u32[]{:S(2)}, u32[]{:S(2)}) %collective-permute-start.5) | collective-permute-done | bytes 163872 | tf_op jit(solution)/shard_map/ppermute | solution.py:15
  109.9 3.5 %all_gather.46 = bf16[2,160,128]{2,1,0:T(8,128)(2,1)S(1)} all-gather(bf16[1,160,128]{2,1,0:T(8,128)(2,1)S(1)} %pad_maximum_fusion.5), channel_id=1, replica_groups=mesh['layer'=32,'far'=4,'near'=2,'c'=2] {'near'}, dimensions={0}, use_global_device_ids=true | all-gather | bytes 122880 | tf_op jit(solution)/shard_map/all_gather | solution.py:194
  113.6 3.9 %all-gather.1 = bf16[4,160,64]{1,2,0:T(8,128)(2,1)S(1)} all-gather(bf16[2,160,64]{1,2,0:T(8,128)(2,1)S(1)} %copy.6), channel_id=3, replica_groups=mesh['layer'=32,'far'=4,'near'=2,'c'=2] {'c'}, dimensions={0}, use_global_device_ids=true | all-gather | bytes 122880 | tf_op jit(solution)/shard_map/all_gather | solution.py:196
  (33 shorter events, 5.5 us)
Async XLA Ops:
  31.2 6.3 %collective-permute-start = (bf16[8,32,1664]{2,1,0:T(8,128)(2,1)S(1)}, bf16[8,32,1664]{2,1,0:T(8,128)(2,1)S(1)}, u32[]{:S(2)}, u32[]{:S(2)}) collective-permute-start(bf16[8,32,1664]{2,1,0:T(8,128)(2,1)S(1)} %all_to_all.5.mine_ref), channel_id=1, source_target_pairs={{0,1},{1,0},{2,3},{3,2},{4,5},{5,4},{6,7},{7,6},{8,9},{9,8},{10,11... | collective-permute-start | bytes 2555912 | tf_op jit(solution)/shard_map/ppermute | solution.py:19
  39.7 10.1 %collective-permute-start.2 = (bf16[288,512]{1,0:T(8,128)(2,1)S(1)}, bf16[288,512]{1,0:T(8,128)(2,1)S(1)}, u32[]{:S(2)}, u32[]{:S(2)}) collective-permute-start(bf16[288,512]{1,0:T(8,128)(2,1)S(1)} %get-tuple-element.13), channel_id=1, source_target_pairs={{16,0},{32,16},{48,32},{64,48},{80,64},{96,80},{112,96},{128,112},... | collective-permute-start | bytes 884744 | tf_op jit(solution)/shard_map/ppermute | solution.py:15
  43.2 13.1 %collective-permute-start.1 = (bf16[288,512]{1,0:T(8,128)(2,1)S(1)}, bf16[288,512]{1,0:T(8,128)(2,1)S(1)}, u32[]{:S(2)}, u32[]{:S(2)}) collective-permute-start(bf16[288,512]{1,0:T(8,128)(2,1)S(1)} %get-tuple-element.13), channel_id=1, source_target_pairs={{0,16},{16,32},{32,48},{48,64},{64,80},{80,96},{96,112},{112,128},... | collective-permute-start | bytes 884744 | tf_op jit(solution)/shard_map/ppermute | solution.py:15
  66.9 20.3 %collective-permute-start.4 = (bf16[288,512]{1,0:T(8,128)(2,1)S(1)}, bf16[288,512]{1,0:T(8,128)(2,1)S(1)}, u32[]{:S(2)}, u32[]{:S(2)}) collective-permute-start(bf16[288,512]{1,0:T(8,128)(2,1)S(1)} %shard_map.60), channel_id=1, source_target_pairs={{32,0},{48,16},{64,32},{80,48},{96,64},{112,80},{128,96},{144,112}... | collective-permute-start | bytes 884744 | tf_op jit(solution)/shard_map/ppermute | solution.py:15
  68.9 18.7 %collective-permute-start.3 = (bf16[288,512]{1,0:T(8,128)(2,1)S(1)}, bf16[288,512]{1,0:T(8,128)(2,1)S(1)}, u32[]{:S(2)}, u32[]{:S(2)}) collective-permute-start(bf16[288,512]{1,0:T(8,128)(2,1)S(1)} %shard_map.60), channel_id=1, source_target_pairs={{0,32},{16,48},{32,64},{48,80},{64,96},{80,112},{96,128},{112,144}... | collective-permute-start | bytes 884744 | tf_op jit(solution)/shard_map/ppermute | solution.py:15
  99.2 7.9 %collective-permute-start.6 = (bf16[160,512]{1,0:T(8,128)(2,1)S(1)}, bf16[160,512]{1,0:T(8,128)(2,1)S(1)}, u32[]{:S(2)}, u32[]{:S(2)}) collective-permute-start(bf16[160,512]{1,0:T(8,128)(2,1)S(1)} %get-tuple-element.33), channel_id=1, source_target_pairs={{64,0},{80,16},{96,32},{112,48},{128,64},{144,80},{160,96},{176,11... | collective-permute-start | bytes 491528 | tf_op jit(solution)/shard_map/ppermute | solution.py:15
  101.1 8.5 %collective-permute-start.5 = (bf16[160,512]{1,0:T(8,128)(2,1)S(1)}, bf16[160,512]{1,0:T(8,128)(2,1)S(1)}, u32[]{:S(2)}, u32[]{:S(2)}) collective-permute-start(bf16[160,512]{1,0:T(8,128)(2,1)S(1)} %get-tuple-element.32), channel_id=1, source_target_pairs={{0,64},{16,80},{32,96},{48,112},{64,128},{80,144},{96,160},{112,17... | collective-permute-start | bytes 491528 | tf_op jit(solution)/shard_map/ppermute | solution.py:15

commit v5 on v4

--- a/solution.py
+++ b/solution.py
@@ -80,7 +80,7 @@
         @pl.when(core_ref[0] == own)
         def _(own=own):
             for k in range(4):
-                turned = done_ref[k // 2, k % 2].astype(jnp.float32).T
+                turned = done_ref[k % 2, k // 2].astype(jnp.float32).T
                 turned = turned[own * n : own * n + n].astype(jnp.bfloat16)
                 diag_ref[0, :, k * q : k * q + q] = turned[:, :q]
                 rhs_ref[0, :, k * g : k * g + g] = turned[:, q:]
@@ -191,10 +191,11 @@
     new_diag = rows_of(diag).astype(jnp.float32) - left[g:] - right[:q]
     new_rhs = rows_of(rhs).astype(jnp.float32) - left[:g] - right[q:]
     done = jnp.concatenate([new_diag, new_rhs], axis=0).astype(jnp.bfloat16)
-    done = lax.all_gather(done, "near", axis=0)
-    done = jnp.where(near == 0, done[:, :, : 2 * n], done[:, :, 2 * n :])
     done = lax.all_gather(done, "c", axis=0)
-    return finish(done, core, n, m, r)
+    low = jnp.concatenate([done[..., :n], done[..., 2 * n : 3 * n]], axis=-1)
+    high = jnp.concatenate([done[..., n : 2 * n], done[..., 3 * n :]], axis=-1)
+    done = lax.all_gather(jnp.where(core == 0, low, high), "near", axis=0)
+    return finish(done, near, n, m, r)
 
 
 def solution(mesh):

time: 119 us -> 119 us (level)
  the two profiles are of different devices: /device:TPU:257 before, /device:TPU:256 now
where the time goes in v5:
time: 119 us
  blocking collectives  70.7 us (59%)
  starting transfers between devices  20.9 us (18%)
  waiting for transfers between devices  17.1 us (14%)
  Pallas kernels  5.32 us (4%)
  matrix products  1.67 us (1%)
  other arithmetic  1.42 us (1%)
    all_to_all x1, blocking collectives, first_solve(): mine = lax.all_to_all(copies, ('far', 'near'), 0, 0, tiled=True)  31.4 us
    ppermute x6, starting transfers between devices, send(): return lax.ppermute(block, 'layer', pairs)  19 us
    ppermute x6, waiting for transfers between devices, send(): return lax.ppermute(block, 'layer', pairs)  14.8 us
    all_gather x2, blocking collectives, of_pair(): return lax.all_gather(rows, 'near', axis=0, tiled=True)  13.3 us
    all_gather x5, blocking collectives, of_cores(): return lax.all_gather(rows, 'c', axis=0, tiled=True)  10.7 us
    all_gather x1, blocking collectives, on_device(): lax.all_gather(jnp.concatenate([lower, upper], axis=0), 'near', axis=0)  8.47 us
    all_gather x1, blocking collectives, on_device(): done = lax.all_gather(jnp.where(core == 0, low, high), 'near', axis=0)  4.94 us
  transfers between devices with their start and end apart: 7, of which 5 were waited for; matrix products, arithmetic and copies ran while one was open for 1% of the time, Pallas kernels for 0%

profile of v5, /device:TPU:256, one launch (start us, length us, event | category | flops | bytes accessed | tf_op | source)
XLA Modules:
  0.0 118.5 jit_solution(17910974860893744932)
XLA Ops:
  1.5 31.4 %all_to_all.5.mine_ref = bf16[8,32,1664]{2,1,0:T(8,128)(2,1)S(1)} all-to-all(bf16[8,32,1664]{2,1,0:T(8,128)(2,1)S(1)} %broadcast_in_dim.2), channel_id=1, replica_groups=mesh['layer'=32,'far'=4,'near'=2,'c'=2] {'far','near'}, dimensions={0} | all-to-all | bytes 1703936 | tf_op jit(solution)/shard_map/all_to_all | solution.py:145
  32.9 1.9 %collective-permute-start = (bf16[8,32,1664]{2,1,0:T(8,128)(2,1)S(1)}, bf16[8,32,1664]{2,1,0:T(8,128)(2,1)S(1)}, u32[]{:S(2)}, u32[]{:S(2)}) collective-permute-start(bf16[8,32,1664]{2,1,0:T(8,128)(2,1)S(1)} %all_to_all.5.mine_ref), channel_id=1, source_target_pairs={{0,1},{1,0},{2,3},{3,2},{4,5},{5,4},{6,7},{7,6},{8,9},{9,8},{10,11... | collective-permute-start | bytes 2555912 | tf_op jit(solution)/shard_map/ppermute | solution.py:19
  34.9 2.3 %collective-permute-done.other_ref = bf16[8,32,1664]{2,1,0:T(8,128)(2,1)S(1)} collective-permute-done((bf16[8,32,1664]{2,1,0:T(8,128)(2,1)S(1)}, bf16[8,32,1664]{2,1,0:T(8,128)(2,1)S(1)}, u32[]{:S(2)}, u32[]{:S(2)}) %collective-permute-start) | collective-permute-done | bytes 852000 | tf_op jit(solution)/shard_map/ppermute | solution.py:19
  37.2 2.2 %shard_map.59 = (bf16[288,512]{1,0:T(8,128)(2,1)S(1)}, bf16[512,512]{1,0:T(8,128)(2,1)S(1)}, bf16[512,512]{1,0:T(8,128)(2,1)S(1)}, bf16[128,512]{1,0:T(8,128)(2,1)S(1)}, bf16[32,512]{1,0:T(8,128)(2,1)S(1)}) custom-call(s32[2]{0:T(128)S(1)} %pad_add_fusion.core_ref, bf16[8,32,1664]{2,1,0:T(8,128)(2,1)S(1)} %all_to_all.5.mine_ref, ...), custom_call_target="tpu_custom_call" | custom-call | flops 939524096 | bytes 4194304 | tf_op jit(solution)/shard_map/pallas_call | solution.py:149
  39.4 3.8 %collective-permute-start.2 = (bf16[288,512]{1,0:T(8,128)(2,1)S(1)}, bf16[288,512]{1,0:T(8,128)(2,1)S(1)}, u32[]{:S(2)}, u32[]{:S(2)}) collective-permute-start(bf16[288,512]{1,0:T(8,128)(2,1)S(1)} %get-tuple-element.13), channel_id=1, source_target_pairs={{16,0},{32,16},{48,32},{64,48},{80,64},{96,80},{112,96},{128,112},... | collective-permute-start | bytes 884744 | tf_op jit(solution)/shard_map/ppermute | solution.py:15
  43.1 2.1 %collective-permute-start.1 = (bf16[288,512]{1,0:T(8,128)(2,1)S(1)}, bf16[288,512]{1,0:T(8,128)(2,1)S(1)}, u32[]{:S(2)}, u32[]{:S(2)}) collective-permute-start(bf16[288,512]{1,0:T(8,128)(2,1)S(1)} %get-tuple-element.13), channel_id=1, source_target_pairs={{0,16},{16,32},{32,48},{48,64},{64,80},{80,96},{96,112},{112,128},... | collective-permute-start | bytes 884744 | tf_op jit(solution)/shard_map/ppermute | solution.py:15
  45.2 5.1 %collective-permute-done.2 = bf16[288,512]{1,0:T(8,128)(2,1)S(1)} collective-permute-done((bf16[288,512]{1,0:T(8,128)(2,1)S(1)}, bf16[288,512]{1,0:T(8,128)(2,1)S(1)}, u32[]{:S(2)}, u32[]{:S(2)}) %collective-permute-start.2) | collective-permute-done | bytes 294944 | tf_op jit(solution)/shard_map/ppermute | solution.py:15
  50.7 6.5 %collective-permute-done.1 = bf16[288,512]{1,0:T(8,128)(2,1)S(1)} collective-permute-done((bf16[288,512]{1,0:T(8,128)(2,1)S(1)}, bf16[288,512]{1,0:T(8,128)(2,1)S(1)}, u32[]{:S(2)}, u32[]{:S(2)}) %collective-permute-start.1) | collective-permute-done | bytes 294944 | tf_op jit(solution)/shard_map/ppermute | solution.py:15
  57.6 5.6 %all_gather.35 = bf16[256,512]{1,0:T(8,128)(2,1)S(1)} all-gather(bf16[128,512]{1,0:T(8,128)(2,1)S(1)} %get-tuple-element.26), channel_id=1, replica_groups=mesh['layer'=32,'far'=4,'near'=2,'c'=2] {'near'}, dimensions={0}, use_global_device_ids=true | all-gather | bytes 393216 | tf_op jit(solution)/shard_map/all_gather | solution.py:27
  63.3 2.2 %all_gather.36.diag_ref = bf16[512,512]{1,0:T(8,128)(2,1)S(1)} all-gather(bf16[256,512]{1,0:T(8,128)(2,1)S(1)} %all_gather.35), channel_id=1, replica_groups=mesh['layer'=32,'far'=4,'near'=2,'c'=2] {'c'}, dimensions={0}, use_global_device_ids=true | all-gather | bytes 786432 | tf_op jit(solution)/shard_map/all_gather | solution.py:23
  65.4 1.2 shard_map.60
  66.6 1.9 %collective-permute-start.4 = (bf16[288,512]{1,0:T(8,128)(2,1)S(1)}, bf16[288,512]{1,0:T(8,128)(2,1)S(1)}, u32[]{:S(2)}, u32[]{:S(2)}) collective-permute-start(bf16[288,512]{1,0:T(8,128)(2,1)S(1)} %shard_map.60), channel_id=1, source_target_pairs={{32,0},{48,16},{64,32},{80,48},{96,64},{112,80},{128,96},{144,112}... | collective-permute-start | bytes 884744 | tf_op jit(solution)/shard_map/ppermute | solution.py:15
  68.6 5.4 %collective-permute-start.3 = (bf16[288,512]{1,0:T(8,128)(2,1)S(1)}, bf16[288,512]{1,0:T(8,128)(2,1)S(1)}, u32[]{:S(2)}, u32[]{:S(2)}) collective-permute-start(bf16[288,512]{1,0:T(8,128)(2,1)S(1)} %shard_map.60), channel_id=1, source_target_pairs={{0,32},{16,48},{32,64},{48,80},{64,96},{80,112},{96,128},{112,144}... | collective-permute-start | bytes 884744 | tf_op jit(solution)/shard_map/ppermute | solution.py:15
  74.0 8.5 %all-gather = bf16[512,512]{1,0:T(8,128)(2,1)S(1)} all-gather(bf16[256,512]{1,0:T(8,128)(2,1)S(1)} %pad_maximum_fusion), channel_id=2, replica_groups=mesh['layer'=32,'far'=4,'near'=2,'c'=2] {'near'}, dimensions={0}, use_global_device_ids=true | all-gather | bytes 786432 | tf_op jit(solution)/shard_map/all_gather | solution.py:173
  82.6 2.2 %all_gather.39 = bf16[512,512]{1,0:T(8,128)(2,1)S(1)} all-gather(bf16[256,512]{1,0:T(8,128)(2,1)S(1)} %pad_maximum_fusion.1), channel_id=1, replica_groups=mesh['layer'=32,'far'=4,'near'=2,'c'=2] {'c'}, dimensions={0}, use_global_device_ids=true | all-gather | bytes 786432 | tf_op jit(solution)/shard_map/all_gather | solution.py:23
  84.8 2.2 %all_gather.40 = bf16[512,512]{1,0:T(8,128)(2,1)S(1)} all-gather(bf16[256,512]{1,0:T(8,128)(2,1)S(1)} %pad_maximum_fusion.2), channel_id=1, replica_groups=mesh['layer'=32,'far'=4,'near'=2,'c'=2] {'c'}, dimensions={0}, use_global_device_ids=true | all-gather | bytes 786432 | tf_op jit(solution)/shard_map/all_gather | solution.py:23
  87.8 7.6 %all_gather.41 = bf16[256,768]{1,0:T(8,128)(2,1)S(1)} all-gather(bf16[128,768]{1,0:T(8,128)(2,1)S(1)} %pad_maximum_fusion.3), channel_id=1, replica_groups=mesh['layer'=32,'far'=4,'near'=2,'c'=2] {'near'}, dimensions={0}, use_global_device_ids=true | all-gather | bytes 589824 | tf_op jit(solution)/shard_map/all_gather | solution.py:27
  95.5 2.2 %all_gather.42.diag_ref = bf16[512,512]{1,0:T(8,128)(2,1)S(1)} all-gather(bf16[256,512]{1,0:T(8,128)(2,1)S(1)} %slice.134), channel_id=1, replica_groups=mesh['layer'=32,'far'=4,'near'=2,'c'=2] {'c'}, dimensions={0}, use_global_device_ids=true | all-gather | bytes 786432 | tf_op jit(solution)/shard_map/all_gather | solution.py:23
  98.9 1.9 %collective-permute-start.6 = (bf16[160,512]{1,0:T(8,128)(2,1)S(1)}, bf16[160,512]{1,0:T(8,128)(2,1)S(1)}, u32[]{:S(2)}, u32[]{:S(2)}) collective-permute-start(bf16[160,512]{1,0:T(8,128)(2,1)S(1)} %get-tuple-element.33), channel_id=1, source_target_pairs={{64,0},{80,16},{96,32},{112,48},{128,64},{144,80},{160,96},{176,11... | collective-permute-start | bytes 491528 | tf_op jit(solution)/shard_map/ppermute | solution.py:15
  100.8 3.9 %collective-permute-start.5 = (bf16[160,512]{1,0:T(8,128)(2,1)S(1)}, bf16[160,512]{1,0:T(8,128)(2,1)S(1)}, u32[]{:S(2)}, u32[]{:S(2)}) collective-permute-start(bf16[160,512]{1,0:T(8,128)(2,1)S(1)} %get-tuple-element.32), channel_id=1, source_target_pairs={{0,64},{16,80},{32,96},{48,112},{64,128},{80,144},{96,160},{112,17... | collective-permute-start | bytes 491528 | tf_op jit(solution)/shard_map/ppermute | solution.py:15
  104.7 2.0 %all_gather.43 = bf16[512,256]{1,0:T(8,128)(2,1)S(1)} all-gather(bf16[256,256]{1,0:T(8,128)(2,1)S(1)} %slice.137), channel_id=1, replica_groups=mesh['layer'=32,'far'=4,'near'=2,'c'=2] {'c'}, dimensions={0}, use_global_device_ids=true | all-gather | bytes 393216 | tf_op jit(solution)/shard_map/all_gather | solution.py:23
  107.2 3.0 %collective-permute-done.5 = bf16[160,512]{1,0:T(8,128)(2,1)S(1)} collective-permute-done((bf16[160,512]{1,0:T(8,128)(2,1)S(1)}, bf16[160,512]{1,0:T(8,128)(2,1)S(1)}, u32[]{:S(2)}, u32[]{:S(2)}) %collective-permute-start.5) | collective-permute-done | bytes 163872 | tf_op jit(solution)/shard_map/ppermute | solution.py:15
  110.4 1.9 %all_gather.44 = bf16[2,160,128]{2,1,0:T(8,128)(2,1)S(1)} all-gather(bf16[1,160,128]{2,1,0:T(8,128)(2,1)S(1)} %pad_maximum_fusion.5), channel_id=1, replica_groups=mesh['layer'=32,'far'=4,'near'=2,'c'=2] {'c'}, dimensions={0}, use_global_device_ids=true | all-gather | bytes 122880 | tf_op jit(solution)/shard_map/all_gather | solution.py:194
  112.6 4.9 %all_gather.45 = bf16[2,2,160,64]{2,3,1,0:T(8,128)(2,1)S(1)} all-gather(bf16[1,2,160,64]{2,3,1,0:T(8,128)(2,1)S(1)} %copy.6), channel_id=1, replica_groups=mesh['layer'=32,'far'=4,'near'=2,'c'=2] {'near'}, dimensions={0}, use_global_device_ids=true | all-gather | bytes 122880 | tf_op jit(solution)/shard_map/all_gather | solution.py:197
  (34 shorter events, 5.9 us)
Async XLA Ops:
  32.9 4.3 %collective-permute-start = (bf16[8,32,1664]{2,1,0:T(8,128)(2,1)S(1)}, bf16[8,32,1664]{2,1,0:T(8,128)(2,1)S(1)}, u32[]{:S(2)}, u32[]{:S(2)}) collective-permute-start(bf16[8,32,1664]{2,1,0:T(8,128)(2,1)S(1)} %all_to_all.5.mine_ref), channel_id=1, source_target_pairs={{0,1},{1,0},{2,3},{3,2},{4,5},{5,4},{6,7},{7,6},{8,9},{9,8},{10,11... | collective-permute-start | bytes 2555912 | tf_op jit(solution)/shard_map/ppermute | solution.py:19
  39.4 11.0 %collective-permute-start.2 = (bf16[288,512]{1,0:T(8,128)(2,1)S(1)}, bf16[288,512]{1,0:T(8,128)(2,1)S(1)}, u32[]{:S(2)}, u32[]{:S(2)}) collective-permute-start(bf16[288,512]{1,0:T(8,128)(2,1)S(1)} %get-tuple-element.13), channel_id=1, source_target_pairs={{16,0},{32,16},{48,32},{64,48},{80,64},{96,80},{112,96},{128,112},... | collective-permute-start | bytes 884744 | tf_op jit(solution)/shard_map/ppermute | solution.py:15
  43.1 14.0 %collective-permute-start.1 = (bf16[288,512]{1,0:T(8,128)(2,1)S(1)}, bf16[288,512]{1,0:T(8,128)(2,1)S(1)}, u32[]{:S(2)}, u32[]{:S(2)}) collective-permute-start(bf16[288,512]{1,0:T(8,128)(2,1)S(1)} %get-tuple-element.13), channel_id=1, source_target_pairs={{0,16},{16,32},{32,48},{48,64},{64,80},{80,96},{96,112},{112,128},... | collective-permute-start | bytes 884744 | tf_op jit(solution)/shard_map/ppermute | solution.py:15
  66.6 20.3 %collective-permute-start.4 = (bf16[288,512]{1,0:T(8,128)(2,1)S(1)}, bf16[288,512]{1,0:T(8,128)(2,1)S(1)}, u32[]{:S(2)}, u32[]{:S(2)}) collective-permute-start(bf16[288,512]{1,0:T(8,128)(2,1)S(1)} %shard_map.60), channel_id=1, source_target_pairs={{32,0},{48,16},{64,32},{80,48},{96,64},{112,80},{128,96},{144,112}... | collective-permute-start | bytes 884744 | tf_op jit(solution)/shard_map/ppermute | solution.py:15
  68.6 18.7 %collective-permute-start.3 = (bf16[288,512]{1,0:T(8,128)(2,1)S(1)}, bf16[288,512]{1,0:T(8,128)(2,1)S(1)}, u32[]{:S(2)}, u32[]{:S(2)}) collective-permute-start(bf16[288,512]{1,0:T(8,128)(2,1)S(1)} %shard_map.60), channel_id=1, source_target_pairs={{0,32},{16,48},{32,64},{48,80},{64,96},{80,112},{96,128},{112,144}... | collective-permute-start | bytes 884744 | tf_op jit(solution)/shard_map/ppermute | solution.py:15
  98.9 8.1 %collective-permute-start.6 = (bf16[160,512]{1,0:T(8,128)(2,1)S(1)}, bf16[160,512]{1,0:T(8,128)(2,1)S(1)}, u32[]{:S(2)}, u32[]{:S(2)}) collective-permute-start(bf16[160,512]{1,0:T(8,128)(2,1)S(1)} %get-tuple-element.33), channel_id=1, source_target_pairs={{64,0},{80,16},{96,32},{112,48},{128,64},{144,80},{160,96},{176,11... | collective-permute-start | bytes 491528 | tf_op jit(solution)/shard_map/ppermute | solution.py:15
  100.8 9.4 %collective-permute-start.5 = (bf16[160,512]{1,0:T(8,128)(2,1)S(1)}, bf16[160,512]{1,0:T(8,128)(2,1)S(1)}, u32[]{:S(2)}, u32[]{:S(2)}) collective-permute-start(bf16[160,512]{1,0:T(8,128)(2,1)S(1)} %get-tuple-element.32), channel_id=1, source_target_pairs={{0,64},{16,80},{32,96},{48,112},{64,128},{80,144},{96,160},{112,17... | collective-permute-start | bytes 491528 | tf_op jit(solution)/shard_map/ppermute | solution.py:15
